TPU v7x, 32 devices: a whole 2x2x4 slice. The times are simulated.
32 devices in a mesh: beam: 2 (over y), freq: 8 (over z, x), tm: 2 (over core).
Axes of the slice: x: 2, y: 2, z: 4, core: 2. Of those that a mesh axis runs over, the one named last changes fastest.
Arguments:
- spectra: float32 [256, 16384], P(('beam', 'freq'), 'tm'), parts along dimension 0, may hold values from -250 to 250
- local_delays: int32 [4, 3, 128], P(None, None, 'freq'), may hold values from 0 to 8, as said below
- merge_delays: int32 [3, 3, 128], P(None, None, 'freq'), may hold values from 0 to 64, as said below
- widths: int32 [16], replicated, may hold values from 1 to 32, as said below
Outputs:
- detections: float32 [256, 16384], P(('beam', 'freq'), 'tm'), parts along dimension 0
There are 2 independent parts, one for each index of `beam`. A program takes and returns all parts, laid end to end along the dimension named above; an argument that names none is the same for every part. Nothing has to cross between parts.
Inputs may be any that keep to these rules, and one draw needn't show every extreme that they name: `local_delays`: entries [s, 0, r] and [s, 1, r] lie in 0 to 2**s - 1, entry [s, 2, r] in 0 to 2**s, and [s, 2, 0] equals 2**s. `merge_delays`: entries [j, 0, r] and [j, 1, r] lie in 0 to 15, entry [j, 2, r] in 0 to 16 * 2**j, and [j, 2, 0] equals 16 * 2**j. 16 distinct widths, one of them 32.
All inputs are finite; a program needn't handle non-finite values.
Results may differ from a plain program's by a relative error of at most 0.00002.
Values sent between devices are 32-bit elements; how exact they have to be, the bound alone decides.
No kernel may reach another device: no remote copies, remote signals or barrier semaphores. Data moves between devices by JAX's collectives and lax.ppermute only.
A program may use at most 64 MiB of HBM per device.

v0:
```python
import math

import jax
import jax.numpy as jnp
from jax import lax
from jax.sharding import PartitionSpec as P

WMAX = 32


EPSILON = 1e-05


def from_behind(value, axis, by):
    size = lax.axis_size(axis)
    pairs = [(i, i + by) for i in range(size) if 0 <= i + by < size]
    return lax.ppermute(value, axis, pairs)


def partner_2(value, axis, bit):
    mask = 2**bit
    pairs = [(source, source ^ mask) for source in range(lax.axis_size(axis))]
    return lax.ppermute(value, axis, pairs)


def shift_rows(signal, delays, length, largest):
    bit_count = largest.bit_length()
    needed = length + 2**bit_count - 1
    current = jnp.pad(signal, ((0, 0), (0, max(0, needed - signal.shape[1]))))
    for bit_num in reversed(range(bit_count)):
        step = 2**bit_num
        new_len = length + step - 1
        taken = (delays // step % 2 == 1)[:, None]
        current = jnp.where(taken, current[:, step : step + new_len], current[:, :new_len])
    return current


def per_device(spectra, local_delays, merge_delays, widths):
    channels, block_len = spectra.shape
    sample_total = block_len * lax.axis_size("tm")
    freq_count = lax.axis_size("freq")
    totals = lax.psum(jnp.sum(spectra, axis=1, keepdims=True), "tm")
    centered = spectra - totals / sample_total
    spread = lax.psum(jnp.sum(centered * centered, axis=1, keepdims=True), "tm")
    series = centered / jnp.sqrt(spread / sample_total + EPSILON)
    reach = channels * freq_count - 1 + WMAX - 1
    leading = from_behind(series[:, :reach], "tm", -1)
    series = jnp.concatenate([series, leading], axis=1)
    row_ids = jnp.arange(channels, dtype=jnp.int32)
    for level_num in range(channels.bit_length() - 1):
        level_size = 2**level_num
        base_row = row_ids // (2 * level_size) * (2 * level_size)
        low_rows = series[base_row + local_delays[level_num, 0]]
        high_rows = series[base_row + level_size + local_delays[level_num, 1]]
        keep_len = series.shape[1] - level_size
        series = low_rows[:, :keep_len] + shift_rows(
            high_rows, local_delays[level_num, 2], keep_len, level_size
        )
    for level_num in range(freq_count.bit_length() - 1):
        stride = 2**level_num
        span = channels * stride
        is_upper = lax.axis_index("freq") // stride % 2 == 1
        low_pick = merge_delays[level_num, 0]
        high_pick = merge_delays[level_num, 1]
        partner = partner_2(series, "freq", level_num)
        low_rows = jnp.where(is_upper, partner[low_pick], series[low_pick])
        high_rows = jnp.where(is_upper, series[high_pick], partner[high_pick])
        keep_len = series.shape[1] - span
        series = low_rows[:, :keep_len] + shift_rows(
            high_rows, merge_delays[level_num, 2], keep_len, span
        )
    running = jnp.zeros((channels, block_len), jnp.float32)
    strongest = jnp.full((channels, block_len), -jnp.inf, jnp.float32)
    for offset in range(WMAX):
        running = running + series[:, offset : offset + block_len]
        chosen = jnp.any(widths == offset + 1)
        strongest = jnp.where(
            chosen, jnp.maximum(strongest, running * (1.0 / math.sqrt(offset + 1))), strongest
        )
    return strongest * (1.0 / math.sqrt(channels * freq_count))


def solution(mesh):
    placed = (P(("beam", "freq"), "tm"), P(None, None, "freq"), P(None, None, "freq"), P())
    return jax.shard_map(
        per_device, mesh=mesh, in_specs=placed, out_specs=P(("beam", "freq"), "tm"), check_vma=False
    )
```

profile of v0, /device:TPU:0, one launch (start us, length us, event | category | flops | bytes accessed | tf_op | source)
XLA Modules:
  0.0 106.1 jit_solution(16173300033060606930)
XLA Ops:
  0.0 1.3 %reduce_sum.18 = f32[16]{0:T(128)S(1)} reduce(f32[16,8192]{1,0:T(8,128)} %param.4, f32[]{:T(128)} %constant.554.clone.1), dimensions={1}, to_apply=%region_32.33 | reduce | flops 131056 | bytes 524356 | tf_op jit(solution)/shard_map/reduce_sum | solution.py:42
  1.3 2.6 %psum.14 = f32[16,1]{0,1:T(1,128)S(1)} all-reduce(f32[16,1]{0,1:T(1,128)S(1)} %bitcast.265), channel_id=1, replica_groups=mesh['beam'=2,'freq'=8,'tm'=2] {'tm'}, use_global_device_ids=true, to_apply=%region_33.34 | all-reduce | flops 16 | bytes 128 | tf_op jit(solution)/shard_map/psum | solution.py:42
  3.9 0.3 multiply_reduce_fusion
  4.1 2.5 %psum.15 = f32[16,1]{0,1:T(1,128)S(1)} all-reduce(f32[16,1]{0,1:T(1,128)S(1)} %bitcast.266), channel_id=1, replica_groups=mesh['beam'=2,'freq'=8,'tm'=2] {'tm'}, use_global_device_ids=true, to_apply=%region_35.36 | all-reduce | flops 16 | bytes 128 | tf_op jit(solution)/shard_map/psum | solution.py:44
  6.8 1.3 %collective-permute-start = (f32[16,158]{1,0:T(8,128)S(1)}, f32[16,158]{1,0:T(8,128)S(1)}, u32[]{:S(2)}, u32[]{:S(2)}) collective-permute-start(f32[16,158]{1,0:T(8,128)S(1)} %slice.514), channel_id=1, source_target_pairs={{1,0},{3,2},{5,4},{7,6},{9,8},{11,10},{13,12},{15,14},{17,16},{19,... | collective-permute-start | bytes 30344 | tf_op jit(solution)/shard_map/ppermute | solution.py:17
  8.3 1.6 %collective-permute-done = f32[16,158]{1,0:T(8,128)S(1)} collective-permute-done((f32[16,158]{1,0:T(8,128)S(1)}, f32[16,158]{1,0:T(8,128)S(1)}, u32[]{:S(2)}, u32[]{:S(2)}) %collective-permute-start) | collective-permute-done | bytes 10144 | tf_op jit(solution)/shard_map/ppermute | solution.py:17
  9.9 0.7 gather_fusion
  10.6 0.7 gather_fusion.1
  11.4 0.2 fusion.3
  11.6 0.7 gather_fusion.3
  12.3 0.7 gather_fusion.2
  13.1 0.2 slice_select_fusion.11
  13.3 0.2 fusion.2
  13.5 0.7 gather_fusion.5
  14.2 0.7 gather_fusion.4
  15.0 0.2 slice_select_fusion.9
  15.2 0.2 slice_select_fusion.8
  15.4 0.2 fusion.1
  15.6 0.7 gather_fusion.7
  16.3 0.7 gather_fusion.6
  17.1 0.2 slice_select_fusion.6
  17.3 0.2 slice_select_fusion.5
  17.7 0.2 fusion
  17.9 2.9 %collective-permute-start.1 = (f32[16,8335]{1,0:T(8,128)S(1)}, f32[16,8335]{1,0:T(8,128)S(1)}, u32[]{:S(2)}, u32[]{:S(2)}) collective-permute-start(f32[16,8335]{1,0:T(8,128)S(1)} %fusion), channel_id=1, source_target_pairs={{0,2},{2,0},{4,6},{6,4},{8,10},{10,8},{12,14},{14,12},{1,3},{3,1},... | collective-permute-start | bytes 1600328 | tf_op jit(solution)/shard_map/ppermute | solution.py:23
  20.9 0.7 gather_fusion.10
  21.7 0.7 gather_fusion.9
  22.4 11.0 %collective-permute-done.1 = f32[16,8335]{1,0:T(8,128)S(1)} collective-permute-done((f32[16,8335]{1,0:T(8,128)S(1)}, f32[16,8335]{1,0:T(8,128)S(1)}, u32[]{:S(2)}, u32[]{:S(2)}) %collective-permute-start.1) | collective-permute-done | bytes 533472 | tf_op jit(solution)/shard_map/ppermute | solution.py:23
  33.4 0.7 gather_fusion.11
  34.2 0.2 slice_select_fusion.2
  35.1 0.7 gather_fusion.8
  35.8 0.2 fusion.8
  36.0 1.9 %collective-permute-start.2 = (f32[16,8319]{1,0:T(8,128)S(1)}, f32[16,8319]{1,0:T(8,128)S(1)}, u32[]{:S(2)}, u32[]{:S(2)}) collective-permute-start(f32[16,8319]{1,0:T(8,128)S(1)} %fusion.8), channel_id=1, source_target_pairs={{0,4},{2,6},{4,0},{6,2},{8,12},{10,14},{12,8},{14,10},{1,5},{3,7},... | collective-permute-start | bytes 1597256 | tf_op jit(solution)/shard_map/ppermute | solution.py:23
  37.9 0.7 gather_fusion.14
  38.7 0.7 gather_fusion.13
  39.4 10.4 %collective-permute-done.2 = f32[16,8319]{1,0:T(8,128)S(1)} collective-permute-done((f32[16,8319]{1,0:T(8,128)S(1)}, f32[16,8319]{1,0:T(8,128)S(1)}, u32[]{:S(2)}, u32[]{:S(2)}) %collective-permute-start.2) | collective-permute-done | bytes 532448 | tf_op jit(solution)/shard_map/ppermute | solution.py:23
  49.8 0.7 gather_fusion.15
  51.6 0.7 gather_fusion.12
  52.3 0.2 fusion.7
  52.6 2.6 %collective-permute-start.3 = (f32[16,8287]{1,0:T(8,128)S(1)}, f32[16,8287]{1,0:T(8,128)S(1)}, u32[]{:S(2)}, u32[]{:S(2)}) collective-permute-start(f32[16,8287]{1,0:T(8,128)S(1)} %fusion.7), channel_id=1, source_target_pairs={{0,8},{2,10},{4,12},{6,14},{8,0},{10,2},{12,4},{14,6},{1,9},{3,11}... | collective-permute-start | bytes 1591112 | tf_op jit(solution)/shard_map/ppermute | solution.py:23
  55.2 0.6 copy-done.3
  55.8 1.2 %compare_reduce_fusion.31 = (pred[]{:T(512)}, pred[]{:T(512)}, pred[]{:T(512)}, pred[]{:T(512)}, pred[]{:T(512)}, /*index=5*/pred[]{:T(512)}, pred[]{:T(512)}, p...) fusion(s32[16]{0:T(128)S(1)} %copy-done.3), kind=kLoop, calls=%fused_computation.286 | loop fusion | flops 992 | bytes 96 | tf_op jit(solution)/shard_map/reduce_or | solution.py:76
  57.0 0.7 gather_fusion.18
  57.8 0.7 gather_fusion.17
  58.5 19.2 %collective-permute-done.3 = f32[16,8287]{1,0:T(8,128)S(1)} collective-permute-done((f32[16,8287]{1,0:T(8,128)S(1)}, f32[16,8287]{1,0:T(8,128)S(1)}, u32[]{:S(2)}, u32[]{:S(2)}) %collective-permute-start.3) | collective-permute-done | bytes 530400 | tf_op jit(solution)/shard_map/ppermute | solution.py:23
  77.7 0.7 gather_fusion.19
  79.8 0.7 gather_fusion.16
  80.5 0.2 fusion.6
  80.7 25.4 %fusion.9 = f32[16,8192]{1,0:T(8,128)} fusion(f32[16,8223]{1,0:T(8,128)S(1)} %fusion.6, pred[]{:T(512)} %get-tuple-element.35, pred[]{:T(512)} %get-tuple-element.36, pred[]{:T(512)} %get-tuple-element.6, pred[]{:T(512)} %get-tuple-element.7, pred[]{:T(512)} %get-tuple-element.8, pred[]{:T(512)} %get-tuple-element.9, pred[]{:T(512)} %get-tuple-element.10, ...), kind=kLoop, calls=%fused_computation.92 | loop fusion | flops 16515072 | bytes 17301536 | tf_op jit(solution)/shard_map/mul | solution.py:80
  (42 shorter events, 3.7 us)
Async XLA Ops:
  0.0 3.9 %copy-start = (f32[16,8192]{1,0:T(8,128)S(1)}, f32[16,8192]{1,0:T(8,128)}, u32[]{:S(2)}) copy-start(f32[16,8192]{1,0:T(8,128)} %param.4) | copy-start | bytes 1572868
  6.8 1.3 %copy-start.1 = (s32[4,3,16]{2,0,1:T(4,128)S(1)}, s32[4,3,16]{2,0,1:T(4,128)}, u32[]{:S(2)}) copy-start(s32[4,3,16]{2,0,1:T(4,128)} %param.5) | copy-start | bytes 2308
  6.8 3.1 %collective-permute-start = (f32[16,158]{1,0:T(8,128)S(1)}, f32[16,158]{1,0:T(8,128)S(1)}, u32[]{:S(2)}, u32[]{:S(2)}) collective-permute-start(f32[16,158]{1,0:T(8,128)S(1)} %slice.514), channel_id=1, source_target_pairs={{1,0},{3,2},{5,4},{7,6},{9,8},{11,10},{13,12},{15,14},{17,16},{19,... | collective-permute-start | bytes 30344 | tf_op jit(solution)/shard_map/ppermute | solution.py:17
  17.7 3.1 %copy-start.2 = (s32[3,3,16]{2,1,0:T(4,128)S(1)}, s32[3,3,16]{2,1,0:T(4,128)}, u32[]{:S(2)}) copy-start(s32[3,3,16]{2,1,0:T(4,128)} %param.6) | copy-start | bytes 1732
  17.9 15.5 %collective-permute-start.1 = (f32[16,8335]{1,0:T(8,128)S(1)}, f32[16,8335]{1,0:T(8,128)S(1)}, u32[]{:S(2)}, u32[]{:S(2)}) collective-permute-start(f32[16,8335]{1,0:T(8,128)S(1)} %fusion), channel_id=1, source_target_pairs={{0,2},{2,0},{4,6},{6,4},{8,10},{10,8},{12,14},{14,12},{1,3},{3,1},... | collective-permute-start | bytes 1600328 | tf_op jit(solution)/shard_map/ppermute | solution.py:23
  36.0 13.7 %collective-permute-start.2 = (f32[16,8319]{1,0:T(8,128)S(1)}, f32[16,8319]{1,0:T(8,128)S(1)}, u32[]{:S(2)}, u32[]{:S(2)}) collective-permute-start(f32[16,8319]{1,0:T(8,128)S(1)} %fusion.8), channel_id=1, source_target_pairs={{0,4},{2,6},{4,0},{6,2},{8,12},{10,14},{12,8},{14,10},{1,5},{3,7},... | collective-permute-start | bytes 1597256 | tf_op jit(solution)/shard_map/ppermute | solution.py:23
  52.6 25.1 %collective-permute-start.3 = (f32[16,8287]{1,0:T(8,128)S(1)}, f32[16,8287]{1,0:T(8,128)S(1)}, u32[]{:S(2)}, u32[]{:S(2)}) collective-permute-start(f32[16,8287]{1,0:T(8,128)S(1)} %fusion.7), channel_id=1, source_target_pairs={{0,8},{2,10},{4,12},{6,14},{8,0},{10,2},{12,4},{14,6},{1,9},{3,11}... | collective-permute-start | bytes 1591112 | tf_op jit(solution)/shard_map/ppermute | solution.py:23
  55.1 0.7 copy-start.3
where the time goes:
time: 107 us; the launch traced here: 106 us
  waiting for transfers between devices  42.2 us (39%)
  other arithmetic  34.5 us (32%)
  local copies, waits for them, and re-layouts  15.3 us (14%)
  starting transfers between devices  8.64 us (8%)
  blocking collectives  5.05 us (5%)
    ppermute x3, waiting for transfers between devices, partner_2(): return lax.ppermute(value, axis, pairs)  40.6 us
    mul x1, other arithmetic, per_device(): return strongest * (1.0 / math.sqrt(channels * freq_count))  25.4 us
    ppermute x3, starting transfers between devices, partner_2(): return lax.ppermute(value, axis, pairs)  7.35 us
    gather x6, local copies, waits for them, and re-layouts, per_device(): low_rows = jnp.where(is_upper, partner[low_pick], series[low_pick])  4.38 us
    gather x6, local copies, waits for them, and re-layouts, per_device(): high_rows = jnp.where(is_upper, series[high_pick], partner[high_pick])  4.37 us
    select_n x21, other arithmetic, shift_rows(): jnp.where(taken, current[:, step:step + new_len], current[:, :new_len])  4.32 us
    gather x4, local copies, waits for them, and re-layouts, per_device(): high_rows = series[base_row + level_size + local_delays[level_num, 1]]  2.93 us
    gather x4, local copies, waits for them, and re-layouts, per_device(): low_rows = series[base_row + local_delays[level_num, 0]]  2.93 us
  transfers between devices with their start and end apart: 4, of which 4 were waited for; matrix products, arithmetic and copies ran while one was open for 5% of the time, Pallas kernels for 0%

commit v1 on v0

v1 whole, which is shorter than its diff:
```python
import functools
import math

import jax
import jax.numpy as jnp
from jax import lax
from jax.experimental import pallas as pl
from jax.experimental.pallas import tpu as pltpu
from jax.sharding import PartitionSpec as P

WMAX = 32
LANES = 128
EPSILON = 1e-05
SHARES = (2, 3, 3)


def up(value, by):
    return -(-value // by) * by


def swap(value, axis, mask):
    pairs = [(source, source ^ mask) for source in range(lax.axis_size(axis))]
    return lax.ppermute(value, axis, pairs)


def shifted_tile(ref, base, delay, wide, lane):
    if wide:
        base = base + delay // LANES
        delay = delay % LANES
    here = ref[pl.ds(base, 8), :]
    after = ref[pl.ds(base + 1, 8), :]
    return pltpu.roll(jnp.where(lane >= delay, here, after), (LANES - delay) % LANES, 1)


def lanes():
    return lax.broadcasted_iota(jnp.int32, (8, LANES), 1)


class Plan:
    def __init__(self, channels, block_len, freq_count, tm_count):
        self.channels = channels
        self.rows = block_len // LANES
        self.freq_count = freq_count
        self.tm_count = tm_count
        self.local_levels = channels.bit_length() - 1
        self.levels = freq_count.bit_length() - 1
        tiles = self.rows // 8
        total = sum(SHARES)
        ends = [tiles - tiles * sum(SHARES[:i]) // total for i in range(len(SHARES) + 1)]
        self.chunks = [(8 * ends[i + 1], 8 * ends[i]) for i in range(len(SHARES))]
        reach = WMAX - 1
        need = [reach]
        for level in reversed(range(self.levels)):
            reach += channels * 2**level
            need.append(reach)
        self.ext = [-(-r // LANES) for r in reversed(need)]
        self.lead = -(-(reach + channels - 1) // LANES)

    def count(self, c):
        return self.chunks[c][1] - self.chunks[c][0]

    def message_rows(self, c, level):
        return self.channels * (self.count(c) + (self.ext[level] if c == 0 else 0))


def stats_kernel(plan, x_ref, widths_ref, msg_ref, caps_ref):
    ch, rows = plan.channels, plan.rows
    for group in range(ch // 8):
        base = group * rows * 8
        parts = [x_ref[pl.ds(base + 8 * i, 8), :] for i in range(8)]
        for i in range(8, rows):
            parts[i % 8] = parts[i % 8] + x_ref[pl.ds(base + 8 * i, 8), :]
        while len(parts) > 1:
            parts = [a + b for a, b in zip(parts[::2], parts[1::2])]
        mean = jnp.sum(parts[0], axis=1, keepdims=True) * (1.0 / (rows * LANES))
        mean = jnp.broadcast_to(mean, (8, LANES))
        parts = [jnp.zeros((8, LANES), jnp.float32) for _ in range(8)]
        for i in range(rows):
            off = x_ref[pl.ds(base + 8 * i, 8), :] - mean
            parts[i % 8] = parts[i % 8] + off * off
        while len(parts) > 1:
            parts = [a + b for a, b in zip(parts[::2], parts[1::2])]
        spread = jnp.sum(parts[0], axis=1, keepdims=True)
        msg_ref[pl.ds(8 * group, 8), :] = mean
        msg_ref[pl.ds(ch + 8 * group, 8), :] = jnp.broadcast_to(spread, (8, LANES))
        for i in range(plan.lead):
            msg_ref[pl.ds(2 * ch + (group * plan.lead + i) * 8, 8), :] = x_ref[pl.ds(base + 8 * i, 8), :]
    width = lax.broadcasted_iota(jnp.int32, (WMAX, LANES), 0) + 1
    caps = jnp.full((WMAX, LANES), -jnp.inf, jnp.float32)
    for k in range(widths_ref.shape[0]):
        caps = jnp.where(width == widths_ref[k], jnp.inf, caps)
    caps_ref[...] = caps


def local_kernel(plan, stride, x_ref, mine_ref, other_ref, delays_ref, *rest):
    outs, (stat, first, second) = rest[: len(plan.chunks)], rest[len(plan.chunks) :]
    ch, rows, lead = plan.channels, plan.rows, plan.lead
    half = rows * LANES
    mean_a, mean_b = mine_ref[pl.ds(0, ch), :], other_ref[pl.ds(0, ch), :]
    gap = mean_a - mean_b
    spread = mine_ref[pl.ds(ch, ch), :] + other_ref[pl.ds(ch, ch), :] + gap * gap * (half / 2.0)
    stat[pl.ds(0, ch), :] = (mean_a + mean_b) * 0.5
    stat[pl.ds(ch, ch), :] = 1.0 / jnp.sqrt(spread * (1.0 / (2 * half)) + EPSILON)
    last = lax.axis_index("tm") == plan.tm_count - 1
    keep = jnp.where(last, 0.0, 1.0).astype(jnp.float32)

    for r in range(ch):
        group, s = r // 8, r % 8
        mean = jnp.broadcast_to(stat[pl.ds(r, 1), :], (8, LANES))
        gain = jnp.broadcast_to(stat[pl.ds(ch + r, 1), :], (8, LANES))
        for k in range(rows // 8):
            tile = x_ref[pl.ds(group * rows * 8 + 64 * k + s, 8, stride=8), :]
            first[pl.ds(r * stride + 8 * k, 8), :] = (tile - mean) * gain
        for i in range(lead):
            row = other_ref[pl.ds(2 * ch + (group * lead + i) * 8 + s, 1), :]
            first[pl.ds(r * stride + rows + i, 1), :] = (row - mean[:1]) * (gain[:1] * keep)

    lane = lanes()
    source, target = first, second
    for level in range(plan.local_levels):
        size = 2**level
        final = level == plan.local_levels - 1
        tiles = (rows + up(lead, 8)) // 8
        for r in range(ch):
            base = r // (2 * size) * (2 * size)
            low = (base + delays_ref[level, 0, r]) * stride
            high = (base + size + delays_ref[level, 1, r]) * stride
            delay = delays_ref[level, 2, r]
            for k in range(tiles):
                tile = source[pl.ds(pl.multiple_of(low + 8 * k, 8), 8), :] + shifted_tile(
                    source, high + 8 * k, delay, False, lane
                )
                if not final:
                    target[pl.ds(r * stride + 8 * k, 8), :] = tile
                else:
                    put(plan, outs, 0, r, k, tile)
        source, target = target, source


def put(plan, outs, level, r, k, tile):
    for c, (start, stop) in enumerate(plan.chunks):
        if start <= 8 * k < stop:
            outs[c][pl.ds(r * (stop - start) + 8 * k - start, 8), :] = tile
    for i in range(8):
        past = 8 * k + i - plan.rows
        if 0 <= past < plan.ext[level]:
            at = plan.channels * plan.count(0) + past * plan.channels + r
            outs[0][pl.ds(at, 1), :] = tile[i : i + 1]


def gather_rows(plan, c, level, stride, both, own_ref, own_next, got_ref, got_next):
    ch, n = plan.channels, plan.count(c)
    span = ch * 2**level
    for side, (ref, following) in enumerate(((own_ref, own_next), (got_ref, got_next))):
        for r in range(ch):
            at = (side * ch + r) * stride
            for k in range(n // 8):
                both[pl.ds(at + 8 * k, 8), :] = ref[pl.ds(r * n + 8 * k, 8), :]
            if c == 0:
                for i in range(plan.ext[level]):
                    both[pl.ds(at + n + i, 1), :] = ref[pl.ds(ch * n + i * ch + r, 1), :]
            else:
                m = plan.count(c - 1)
                for k in range(up(span // LANES + 1, 8) // 8):
                    both[pl.ds(at + n + 8 * k, 8), :] = following[pl.ds(r * m + 8 * k, 8), :]


def merged_tile(plan, level, stride, both, delays_ref, upper, r, k, lane):
    ch = plan.channels
    low = (jnp.where(upper, ch, 0) + delays_ref[level, 0, r]) * stride + 8 * k
    high = (jnp.where(upper, 0, ch) + delays_ref[level, 1, r]) * stride + 8 * k
    wide = ch * 2**level >= LANES
    return both[pl.ds(pl.multiple_of(low, 8), 8), :] + shifted_tile(
        both, high, delays_ref[level, 2, r], wide, lane
    )


def merge_kernel(plan, c, level, stride, *refs):
    if c == 0:
        own_ref, got_ref, delays_ref, out_ref, both = refs
        own_next = got_next = None
    else:
        own_ref, own_next, got_ref, got_next, delays_ref, out_ref, both = refs
    n = plan.count(c)
    gather_rows(plan, c, level, stride, both, own_ref, own_next, got_ref, got_next)
    upper = lax.axis_index("freq") // 2**level % 2 == 1
    lane = lanes()
    rows = n + (up(plan.ext[level + 1], 8) if c == 0 else 0)
    outs = [None] * len(plan.chunks)
    outs[c] = out_ref
    for r in range(plan.channels):
        for k in range(rows // 8):
            tile = merged_tile(plan, level, stride, both, delays_ref, upper, r, k, lane)
            put(plan, outs, level + 1, r, k + plan.chunks[c][0] // 8, tile)


def final_kernel(plan, c, stride, *refs):
    level = plan.levels - 1
    ch, n = plan.channels, plan.count(c)
    if c == 0:
        own_ref, got_ref, delays_ref, caps_ref, out_ref, head_ref, both, series, box, sem = refs
        own_next = got_next = None
    else:
        (own_ref, own_next, got_ref, got_next, after_ref, delays_ref, caps_ref, _, out_ref, head_ref,
         both, series, box, sem) = refs
    gather_rows(plan, c, level, stride, both, own_ref, own_next, got_ref, got_next)
    upper = lax.axis_index("freq") // 2**level % 2 == 1
    lane = lanes()
    tiles = n // 8
    scale = 1.0 / math.sqrt(ch * plan.freq_count)
    pitch = n + 8
    for r in range(ch):
        for k in range(tiles + (1 if c == 0 else 0)):
            tile = merged_tile(plan, level, stride, both, delays_ref, upper, r, k, lane)
            series[pl.ds(r * pitch + 8 * k, 8), :] = tile
            if k == 0:
                head_ref[pl.ds(r, 1), :] = tile[:1]
        if c > 0:
            series[pl.ds(r * pitch + n, 1), :] = after_ref[pl.ds(r, 1), :]

    def one_row(r, carry):
        at = pl.multiple_of(r * pitch, 8)
        here = [series[pl.ds(at + 8 * k, 8), :] for k in range(tiles)]
        after = [series[pl.ds(at + 8 * k + 1, 8), :] for k in range(tiles)]
        running = here
        best = None
        for offset in range(WMAX):
            if offset:
                running = [
                    total + pltpu.roll(jnp.where(lane >= offset, a, b), LANES - offset, 1)
                    for total, a, b in zip(running, here, after)
                ]
            cap = jnp.broadcast_to(caps_ref[pl.ds(offset, 1), :], (8, LANES))
            factor = scale / math.sqrt(offset + 1)
            value = [jnp.minimum(total * factor, cap) for total in running]
            best = value if best is None else [jnp.maximum(a, b) for a, b in zip(best, value)]
        for k in range(tiles):
            box[pl.ds((r // 8) * (n * 8) + 64 * k + r % 8, 8, stride=8), :] = best[k]
        return carry

    lax.fori_loop(0, ch, one_row, 0)
    start = plan.chunks[c][0]
    copies = [
        pltpu.make_async_copy(
            box.at[pl.ds(group * n * 8, n * 8), :],
            out_ref.at[pl.ds((group * plan.rows + start) * 8, n * 8), :],
            sem.at[group],
        )
        for group in range(ch // 8)
    ]
    for copy in copies:
        copy.start()
    for copy in copies:
        copy.wait()


VMEM = pl.BlockSpec(memory_space=pltpu.VMEM)
SMEM = pl.BlockSpec(memory_space=pltpu.SMEM)
ANY = pl.BlockSpec(memory_space=pl.ANY)


def f32(*shape):
    return jax.ShapeDtypeStruct(shape, jnp.float32)


def call(kernel, ins, specs, outs, out_specs, scratch, ops, aliases=None):
    size = sum(math.prod(o.shape) for o in outs) * 4
    return pl.pallas_call(
        kernel,
        in_specs=specs,
        out_shape=outs,
        out_specs=out_specs,
        scratch_shapes=scratch,
        input_output_aliases=aliases or {},
        cost_estimate=pl.CostEstimate(flops=ops, bytes_accessed=3 * size, transcendentals=0),
        compiler_params=pltpu.CompilerParams(vmem_limit_bytes=24 * 2**20),
    )(*ins)


def per_device(plan, spectra, local_delays, merge_delays, widths):
    ch, rows = plan.channels, plan.rows
    chunks = range(len(plan.chunks))
    x = spectra.reshape(ch // 8, 8, rows, LANES).transpose(0, 2, 1, 3).reshape(ch * rows, LANES)
    msg, caps = call(
        functools.partial(stats_kernel, plan), (x, widths), [VMEM, SMEM],
        [f32(2 * ch + ch * plan.lead, LANES), f32(WMAX, LANES)], [VMEM, VMEM], [], 10**6,
    )
    other = swap(msg, "tm", 1)
    stride = rows + up(plan.lead, 8) + 8
    held = call(
        functools.partial(local_kernel, plan, stride), (x, msg, other, local_delays),
        [VMEM, VMEM, VMEM, SMEM], [f32(plan.message_rows(c, 0), LANES) for c in chunks],
        [VMEM for _ in chunks],
        [pltpu.VMEM((2 * ch, LANES), jnp.float32)] + [pltpu.VMEM((ch * stride, LANES), jnp.float32)] * 2,
        4 * 10**6,
    )
    for level in range(plan.levels):
        got = [swap(held[c], "freq", 2**level) for c in chunks]
        span = ch * 2**level
        made = []
        for c in chunks:
            n = plan.count(c)
            tail = max(up(plan.ext[level + 1], 8) if c == 0 else 0, 0) + span // LANES + 1
            tail = max(tail, plan.ext[level], up(span // LANES + 1, 8))
            stride = up(n + tail, 8)
            both = pltpu.VMEM((2 * ch * stride, LANES), jnp.float32)
            if c == 0:
                ins, specs = [held[0], got[0]], [VMEM] * 2
            else:
                ins, specs = [held[c], held[c - 1], got[c], got[c - 1]], [VMEM] * 4
            if level < plan.levels - 1:
                (out,) = call(
                    functools.partial(merge_kernel, plan, c, level, stride), (*ins, merge_delays),
                    [*specs, SMEM], [f32(plan.message_rows(c, level + 1), LANES)], [VMEM], [both],
                    8 * ch * n * LANES,
                )
                made.append(out)
                continue
            if c > 0:
                ins, specs = [*ins, head], [*specs, VMEM]
            ins, specs = [*ins, merge_delays, caps], [*specs, SMEM, VMEM]
            aliases = {}
            if c > 0:
                aliases = {len(ins): 0}
                ins, specs = [*ins, result], [*specs, ANY]
            result, head = call(
                functools.partial(final_kernel, plan, c, stride), ins, specs,
                [f32(ch * rows, LANES), f32(ch, LANES)], [ANY, VMEM],
                [both, pltpu.VMEM((ch * (n + 8), LANES), jnp.float32),
                 pltpu.VMEM((ch * n, LANES), jnp.float32), pltpu.SemaphoreType.DMA((ch // 8,))],
                200 * ch * n * LANES, aliases,
            )
        held = made
    return result.reshape(ch // 8, rows, 8, LANES).transpose(0, 2, 1, 3).reshape(ch, rows * LANES)


def solution(mesh):
    placed = (P(("beam", "freq"), "tm"), P(None, None, "freq"), P(None, None, "freq"), P())

    def whole(spectra, local_delays, merge_delays, widths):
        channels = spectra.shape[0] // (mesh.shape["beam"] * mesh.shape["freq"])
        block_len = spectra.shape[1] // mesh.shape["tm"]
        plan = Plan(channels, block_len, mesh.shape["freq"], mesh.shape["tm"])
        return jax.shard_map(
            functools.partial(per_device, plan), mesh=mesh, in_specs=placed,
            out_specs=P(("beam", "freq"), "tm"), check_vma=False,
        )(spectra, local_delays, merge_delays, widths)

    return whole
```

time: 107 us -> 74.5 us (0.70)
  other arithmetic: 34.5 us -> 0 us
  Pallas kernels: 0 us -> 20 us
  local copies, waits for them, and re-layouts: 15.3 us -> 1.71 us
  starting transfers between devices: 8.64 us -> 15.1 us
  blocking collectives: 5.05 us -> 0 us
  waiting for transfers between devices: 42.2 us -> 37.4 us
    mul x1 -> x0, other arithmetic: 25.4 us -> none  [per_device(): return strongest * (1.0 / math.sqrt(channels * freq_count))]
    pallas_call x0 -> x11, Pallas kernels: none -> 20 us  [call(): pl.pallas_call(kernel, in_specs=specs, out_shape=outs, out_specs=out_spec...]
    gather x20 -> x0, local copies, waits for them, and re-layouts: 14.6 us -> none  [the longest x6 4.38 us: per_device(): low_rows = jnp.where(is_upper, partner[low_pick], series[low_pick])]
    ppermute x4 -> x10, starting transfers between devices: 8.64 us -> 15.1 us  [swap(): return lax.ppermute(value, axis, pairs)]
    psum x2 -> x0, blocking collectives: 5.05 us -> none  [the longest x1 2.58 us: per_device(): totals = lax.psum(jnp.sum(spectra, axis=1, keepdims=True), 'tm')]
    ppermute x4 -> x10, waiting for transfers between devices: 42.2 us -> 37.4 us  [swap(): return lax.ppermute(value, axis, pairs)]
    select_n x26 -> x0, other arithmetic: 4.53 us -> none  [the longest x21 4.32 us: shift_rows(): jnp.where(taken, current[:, step:step + new_len], current[:, :new_len])]
    reduce_sum x2 -> x0, other arithmetic: 1.56 us -> none  [the longest x1 1.29 us: per_device(): totals = lax.psum(jnp.sum(spectra, axis=1, keepdims=True), 'tm')]
  transfers between devices with their start and end apart: 4 -> 10, of which waited for: 4 -> 4; matrix products, arithmetic and copies ran while one was open for 5% -> 0% of each run, Pallas kernels for 0% -> 17%
where the time goes in v1:
time: 74.5 us; the launch traced here: 74.3 us
  waiting for transfers between devices  37.4 us (50%)
  Pallas kernels  20 us (27%)
  starting transfers between devices  15.1 us (20%)
  local copies, waits for them, and re-layouts  1.71 us (2%)
    ppermute x10, waiting for transfers between devices, swap(): return lax.ppermute(value, axis, pairs)  37.4 us
    pallas_call x11, Pallas kernels, call(): pl.pallas_call(kernel, in_specs=specs, out_shape=outs, out_specs=out_spec...  20 us
    ppermute x10, starting transfers between devices, swap(): return lax.ppermute(value, axis, pairs)  15.1 us
    unnamed x9, local copies, waits for them, and re-layouts  1.71 us
  transfers between devices with their start and end apart: 10, of which 4 were waited for; matrix products, arithmetic and copies ran while one was open for 0% of the time, Pallas kernels for 17%

profile of v1, /device:TPU:0, one launch (start us, length us, event | category | flops | bytes accessed | tf_op | source)
XLA Modules:
  0.0 74.3 jit_solution(4803270275814259231)
XLA Ops:
  0.0 0.0 copy-start.2
  0.0 0.7 copy-done.2
  0.7 0.0 copy-start
  0.7 1.0 %copy-done = f32[16,8192]{1,0:T(8,128)S(1)} copy-done((f32[16,8192]{1,0:T(8,128)S(1)}, f32[16,8192]{1,0:T(8,128)}, u32[]{:S(2)}) %copy-start) | copy-done | bytes 524312
  1.7 0.0 copy-start.3
  1.7 0.8 %shard_map.46 = (f32[64,128]{1,0:T(8,128)S(1)}, f32[32,128]{1,0:T(8,128)S(1)}) custom-call(f32[1024,128]{1,0:T(8,128)S(1)} %bitcast.10, s32[16]{0:T(128)S(1)} %copy-done.2), custom_call_target="tpu_custom_call" | custom-call | flops 1000000 | bytes 147456 | tf_op jit(solution)/shard_map/pallas_call | solution.py:268
  2.5 0.5 collective-permute-start
  2.9 0.0 copy-done.3
  2.9 0.9 %collective-permute-done.other_ref = f32[64,128]{1,0:T(8,128)S(1)} collective-permute-done((f32[64,128]{1,0:T(8,128)S(1)}, f32[64,128]{1,0:T(8,128)S(1)}, u32[]{:S(2)}, u32[]{:S(2)}) %collective-permute-start) | collective-permute-done | bytes 32800 | tf_op jit(solution)/shard_map/ppermute | solution.py:23
  3.8 0.0 copy-start.1
  3.8 1.7 %shard_map.47 = (f32[288,128]{1,0:T(8,128)S(1)}, f32[384,128]{1,0:T(8,128)S(1)}, f32[384,128]{1,0:T(8,128)S(1)}) custom-call(f32[1024,128]{1,0:T(8,128)S(1)} %bitcast.11, f32[64,128]{1,0:T(8,128)S(1)} %get-tuple-element.15.mine_ref, f32[64,128]{1,0:T(8,128)S(1)} %collective-permute-done.other_ref, s32[4,3,16]{2,1,0:T(4,128)S(1)} %copy.7.delays_ref), custom_call_target="tpu_custom_call" | custom-call | flops 4000000 | bytes 1622016 | tf_op jit(solution)/shard_map/pallas_call | solution.py:268
  5.5 2.9 %collective-permute-start.2 = (f32[384,128]{1,0:T(8,128)S(1)}, f32[384,128]{1,0:T(8,128)S(1)}, u32[]{:S(2)}, u32[]{:S(2)}) collective-permute-start(f32[384,128]{1,0:T(8,128)S(1)} %get-tuple-element.17.refs_1_.refs_0_), channel_id=1, source_target_pairs={{0,2},{2,0},{4,6},{6,4},{8,10},{10,8},{12,14},{14,12},{1,3},{3,1},... | collective-permute-start | bytes 589832 | tf_op jit(solution)/shard_map/ppermute | solution.py:23
  8.4 0.1 collective-permute-start.1
  8.5 1.9 %collective-permute-start.3 = (f32[288,128]{1,0:T(8,128)S(1)}, f32[288,128]{1,0:T(8,128)S(1)}, u32[]{:S(2)}, u32[]{:S(2)}) collective-permute-start(f32[288,128]{1,0:T(8,128)S(1)} %get-tuple-element.18.refs_1_.refs_0_), channel_id=1, source_target_pairs={{0,2},{2,0},{4,6},{6,4},{8,10},{10,8},{12,14},{14,12},{1,3},{3,1},... | collective-permute-start | bytes 442376 | tf_op jit(solution)/shard_map/ppermute | solution.py:23
  10.4 10.6 %collective-permute-done.3.refs_3_.refs_1_ = f32[288,128]{1,0:T(8,128)S(1)} collective-permute-done((f32[288,128]{1,0:T(8,128)S(1)}, f32[288,128]{1,0:T(8,128)S(1)}, u32[]{:S(2)}, u32[]{:S(2)}) %collective-permute-start.3) | collective-permute-done | bytes 147488 | tf_op jit(solution)/shard_map/ppermute | solution.py:23
  21.0 0.0 collective-permute-done.2.refs_3_.refs_2_
  21.0 0.0 copy-done.1
  21.0 0.8 %shard_map.49.refs_1_.refs_0_ = f32[384,128]{1,0:T(8,128)S(1)} custom-call(f32[384,128]{1,0:T(8,128)S(1)} %get-tuple-element.17.refs_1_.refs_0_, f32[288,128]{1,0:T(8,128)S(1)} %get-tuple-element.18.refs_1_.refs_0_, f32[384,128]{1,0:T(8,128)S(1)} %collective-permute-done.2.refs_3_.refs_2_, f32[288,128]{1,0:T(8,128)S(1)} %collective-permute-done.3.refs_3_.refs_1_, ...), custom_call_target="tpu_custom_call" | custom-call | flops 393216 | bytes 589824 | tf_op jit(solution)/shard_map/pallas_call | solution.py:268
  21.8 1.9 %collective-permute-start.5 = (f32[384,128]{1,0:T(8,128)S(1)}, f32[384,128]{1,0:T(8,128)S(1)}, u32[]{:S(2)}, u32[]{:S(2)}) collective-permute-start(f32[384,128]{1,0:T(8,128)S(1)} %shard_map.49.refs_1_.refs_0_), channel_id=1, source_target_pairs={{0,4},{2,6},{4,0},{6,2},{8,12},{10,14},{12,8},{14,10},{1,5},{3,7},... | collective-permute-start | bytes 589832 | tf_op jit(solution)/shard_map/ppermute | solution.py:23
  23.7 0.0 collective-permute-done.1.refs_2_
  23.7 0.8 %shard_map.48.refs_0_ = f32[384,128]{1,0:T(8,128)S(1)} custom-call(f32[384,128]{1,0:T(8,128)S(1)} %get-tuple-element.16.refs_0_, f32[384,128]{1,0:T(8,128)S(1)} %get-tuple-element.17.refs_1_.refs_0_, f32[384,128]{1,0:T(8,128)S(1)} %collective-permute-done.1.refs_2_, f32[384,128]{1,0:T(8,128)S(1)} %collective-permute-done.2.refs_3_.refs_2_, ...), custom_call_target="tpu_custom_call" | custom-call | flops 393216 | bytes 589824 | tf_op jit(solution)/shard_map/pallas_call | solution.py:268
  24.5 0.3 collective-permute-start.4
  24.7 0.8 %shard_map.51.refs_1_.refs_0_ = f32[272,128]{1,0:T(8,128)S(1)} custom-call(f32[288,128]{1,0:T(8,128)S(1)} %get-tuple-element.18.refs_1_.refs_0_, f32[288,128]{1,0:T(8,128)S(1)} %collective-permute-done.3.refs_3_.refs_1_, s32[3,3,16]{2,1,0:T(4,128)S(1)} %copy-done.1), custom_call_target="tpu_custom_call" | custom-call | flops 262144 | bytes 417792 | tf_op jit(solution)/shard_map/pallas_call | solution.py:268
  25.6 1.9 %collective-permute-start.6 = (f32[272,128]{1,0:T(8,128)S(1)}, f32[272,128]{1,0:T(8,128)S(1)}, u32[]{:S(2)}, u32[]{:S(2)}) collective-permute-start(f32[272,128]{1,0:T(8,128)S(1)} %shard_map.51.refs_1_.refs_0_), channel_id=1, source_target_pairs={{0,4},{2,6},{4,0},{6,2},{8,12},{10,14},{12,8},{14,10},{1,5},{3,7},... | collective-permute-start | bytes 417800 | tf_op jit(solution)/shard_map/ppermute | solution.py:23
  27.4 8.1 %collective-permute-done.6.refs_3_.refs_1_ = f32[272,128]{1,0:T(8,128)S(1)} collective-permute-done((f32[272,128]{1,0:T(8,128)S(1)}, f32[272,128]{1,0:T(8,128)S(1)}, u32[]{:S(2)}, u32[]{:S(2)}) %collective-permute-start.6) | collective-permute-done | bytes 139296 | tf_op jit(solution)/shard_map/ppermute | solution.py:23
  35.5 0.0 collective-permute-done.5.refs_3_.refs_2_
  35.5 0.8 %shard_map.52.refs_0_.refs_1_ = f32[384,128]{1,0:T(8,128)S(1)} custom-call(f32[384,128]{1,0:T(8,128)S(1)} %shard_map.49.refs_1_.refs_0_, f32[272,128]{1,0:T(8,128)S(1)} %shard_map.51.refs_1_.refs_0_, f32[384,128]{1,0:T(8,128)S(1)} %collective-permute-done.5.refs_3_.refs_2_, f32[272,128]{1,0:T(8,128)S(1)} %collective-permute-done.6.refs_3_.refs_1_, ...), custom_call_target="tpu_custom_call" | custom-call | flops 393216 | bytes 589824 | tf_op jit(solution)/shard_map/pallas_call | solution.py:268
  36.3 2.6 %collective-permute-start.8 = (f32[384,128]{1,0:T(8,128)S(1)}, f32[384,128]{1,0:T(8,128)S(1)}, u32[]{:S(2)}, u32[]{:S(2)}) collective-permute-start(f32[384,128]{1,0:T(8,128)S(1)} %shard_map.52.refs_0_.refs_1_), channel_id=1, source_target_pairs={{0,8},{2,10},{4,12},{6,14},{8,0},{10,2},{12,4},{14,6},{1,9},{3,11}... | collective-permute-start | bytes 589832 | tf_op jit(solution)/shard_map/ppermute | solution.py:23
  38.9 0.0 collective-permute-done.4.refs_2_
  38.9 0.8 %shard_map.50.refs_0_ = f32[384,128]{1,0:T(8,128)S(1)} custom-call(f32[384,128]{1,0:T(8,128)S(1)} %shard_map.48.refs_0_, f32[384,128]{1,0:T(8,128)S(1)} %shard_map.49.refs_1_.refs_0_, f32[384,128]{1,0:T(8,128)S(1)} %collective-permute-done.4.refs_2_, f32[384,128]{1,0:T(8,128)S(1)} %collective-permute-done.5.refs_3_.refs_2_, s32[3,3,16]{2,1,0:T(4,128)S(1)} %copy-done.1), custom_call_target="tpu_custom_call" | custom-call | flops 393216 | bytes 589824 | tf_op jit(solution)/shard_map/pallas_call | solution.py:268
  39.7 0.5 collective-permute-start.7
  40.2 0.8 %shard_map.53.refs_0_.refs_1_ = f32[272,128]{1,0:T(8,128)S(1)} custom-call(f32[272,128]{1,0:T(8,128)S(1)} %shard_map.51.refs_1_.refs_0_, f32[272,128]{1,0:T(8,128)S(1)} %collective-permute-done.6.refs_3_.refs_1_, s32[3,3,16]{2,1,0:T(4,128)S(1)} %copy-done.1), custom_call_target="tpu_custom_call" | custom-call | flops 262144 | bytes 417792 | tf_op jit(solution)/shard_map/pallas_call | solution.py:268
  41.0 2.6 %collective-permute-start.9 = (f32[272,128]{1,0:T(8,128)S(1)}, f32[272,128]{1,0:T(8,128)S(1)}, u32[]{:S(2)}, u32[]{:S(2)}) collective-permute-start(f32[272,128]{1,0:T(8,128)S(1)} %shard_map.53.refs_0_.refs_1_), channel_id=1, source_target_pairs={{0,8},{2,10},{4,12},{6,14},{8,0},{10,2},{12,4},{14,6},{1,9},{3,11}... | collective-permute-start | bytes 417800 | tf_op jit(solution)/shard_map/ppermute | solution.py:23
  43.6 17.9 %collective-permute-done.9.refs_1_.refs_3_ = f32[272,128]{1,0:T(8,128)S(1)} collective-permute-done((f32[272,128]{1,0:T(8,128)S(1)}, f32[272,128]{1,0:T(8,128)S(1)}, u32[]{:S(2)}, u32[]{:S(2)}) %collective-permute-start.9) | collective-permute-done | bytes 139296 | tf_op jit(solution)/shard_map/ppermute | solution.py:23
  61.4 3.7 %shard_map.54 = (f32[1024,128]{1,0:T(8,128)}, f32[16,128]{1,0:T(8,128)S(1)}) custom-call(f32[272,128]{1,0:T(8,128)S(1)} %shard_map.53.refs_0_.refs_1_, f32[272,128]{1,0:T(8,128)S(1)} %collective-permute-done.9.refs_1_.refs_3_, s32[3,3,16]{2,1,0:T(4,128)S(1)} %copy-done.1, f32[32,128]{1,0:T(8,128)S(1)} %get-tuple-element.19.refs_3_.refs_6_), custom_call_target="tpu_custom_call" | custom-call | flops 6553600 | bytes 1597440 | tf_op jit(solution)/shard_map/pallas_call | solution.py:268
  65.1 0.0 collective-permute-done.8.refs_2_.refs_3_
  65.2 4.3 %shard_map.55 = (f32[1024,128]{1,0:T(8,128)}, f32[16,128]{1,0:T(8,128)S(1)}) custom-call(f32[384,128]{1,0:T(8,128)S(1)} %shard_map.52.refs_0_.refs_1_, f32[272,128]{1,0:T(8,128)S(1)} %shard_map.53.refs_0_.refs_1_, f32[384,128]{1,0:T(8,128)S(1)} %collective-permute-done.8.refs_2_.refs_3_, ...), custom_call_target="tpu_custom_call", output_to_operand_aliasing={{0}: (7, {})} | custom-call | flops 9830400 | bytes 1597440 | tf_op jit(solution)/shard_map/pallas_call | solution.py:268
  69.4 0.0 collective-permute-done.7.refs_2_
  69.4 4.9 %shard_map.56 = (f32[1024,128]{1,0:T(8,128)}, f32[16,128]{1,0:T(8,128)}) custom-call(f32[384,128]{1,0:T(8,128)S(1)} %shard_map.50.refs_0_, f32[384,128]{1,0:T(8,128)S(1)} %shard_map.52.refs_0_.refs_1_, f32[384,128]{1,0:T(8,128)S(1)} %collective-permute-done.7.refs_2_, ...), custom_call_target="tpu_custom_call", output_to_operand_aliasing={{0}: (7, {})} | custom-call | flops 9830400 | bytes 1597440 | tf_op jit(solution)/shard_map/pallas_call | solution.py:268
  (1 shorter events, 0.0 us)
Async XLA Ops:
  0.0 0.7 copy-start.2
  0.7 1.0 %copy-start = (f32[16,8192]{1,0:T(8,128)S(1)}, f32[16,8192]{1,0:T(8,128)}, u32[]{:S(2)}) copy-start(f32[16,8192]{1,0:T(8,128)} %param.4) | copy-start | bytes 1572868
  1.7 1.2 %copy-start.3 = (s32[4,3,16]{2,0,1:T(4,128)S(1)}, s32[4,3,16]{2,0,1:T(4,128)}, u32[]{:S(2)}) copy-start(s32[4,3,16]{2,0,1:T(4,128)} %param.5) | copy-start | bytes 2308
  2.5 1.3 %collective-permute-start = (f32[64,128]{1,0:T(8,128)S(1)}, f32[64,128]{1,0:T(8,128)S(1)}, u32[]{:S(2)}, u32[]{:S(2)}) collective-permute-start(f32[64,128]{1,0:T(8,128)S(1)} %get-tuple-element.15.mine_ref), channel_id=1, source_target_pairs={{0,1},{1,0},{2,3},{3,2},{4,5},{5,4},{6,7},{7,6},{8,9},{9,8},{10,11... | collective-permute-start | bytes 98312 | tf_op jit(solution)/shard_map/ppermute | solution.py:23
  3.8 17.2 %copy-start.1 = (s32[3,3,16]{2,1,0:T(4,128)S(1)}, s32[3,3,16]{2,1,0:T(4,128)}, u32[]{:S(2)}) copy-start(s32[3,3,16]{2,1,0:T(4,128)} %refs_5_.3) | copy-start | bytes 1732
  5.5 15.5 %collective-permute-start.2 = (f32[384,128]{1,0:T(8,128)S(1)}, f32[384,128]{1,0:T(8,128)S(1)}, u32[]{:S(2)}, u32[]{:S(2)}) collective-permute-start(f32[384,128]{1,0:T(8,128)S(1)} %get-tuple-element.17.refs_1_.refs_0_), channel_id=1, source_target_pairs={{0,2},{2,0},{4,6},{6,4},{8,10},{10,8},{12,14},{14,12},{1,3},{3,1},... | collective-permute-start | bytes 589832 | tf_op jit(solution)/shard_map/ppermute | solution.py:23
  8.4 15.3 %collective-permute-start.1 = (f32[384,128]{1,0:T(8,128)S(1)}, f32[384,128]{1,0:T(8,128)S(1)}, u32[]{:S(2)}, u32[]{:S(2)}) collective-permute-start(f32[384,128]{1,0:T(8,128)S(1)} %get-tuple-element.16.refs_0_), channel_id=1, source_target_pairs={{0,2},{2,0},{4,6},{6,4},{8,10},{10,8},{12,14},{14,12},{1,3},{3,1},... | collective-permute-start | bytes 589832 | tf_op jit(solution)/shard_map/ppermute | solution.py:23
  8.5 12.5 %collective-permute-start.3 = (f32[288,128]{1,0:T(8,128)S(1)}, f32[288,128]{1,0:T(8,128)S(1)}, u32[]{:S(2)}, u32[]{:S(2)}) collective-permute-start(f32[288,128]{1,0:T(8,128)S(1)} %get-tuple-element.18.refs_1_.refs_0_), channel_id=1, source_target_pairs={{0,2},{2,0},{4,6},{6,4},{8,10},{10,8},{12,14},{14,12},{1,3},{3,1},... | collective-permute-start | bytes 442376 | tf_op jit(solution)/shard_map/ppermute | solution.py:23
  21.8 13.7 %collective-permute-start.5 = (f32[384,128]{1,0:T(8,128)S(1)}, f32[384,128]{1,0:T(8,128)S(1)}, u32[]{:S(2)}, u32[]{:S(2)}) collective-permute-start(f32[384,128]{1,0:T(8,128)S(1)} %shard_map.49.refs_1_.refs_0_), channel_id=1, source_target_pairs={{0,4},{2,6},{4,0},{6,2},{8,12},{10,14},{12,8},{14,10},{1,5},{3,7},... | collective-permute-start | bytes 589832 | tf_op jit(solution)/shard_map/ppermute | solution.py:23
  24.5 14.4 %collective-permute-start.4 = (f32[384,128]{1,0:T(8,128)S(1)}, f32[384,128]{1,0:T(8,128)S(1)}, u32[]{:S(2)}, u32[]{:S(2)}) collective-permute-start(f32[384,128]{1,0:T(8,128)S(1)} %shard_map.48.refs_0_), channel_id=1, source_target_pairs={{0,4},{2,6},{4,0},{6,2},{8,12},{10,14},{12,8},{14,10},{1,5},{3,7},... | collective-permute-start | bytes 589832 | tf_op jit(solution)/shard_map/ppermute | solution.py:23
  25.6 10.0 %collective-permute-start.6 = (f32[272,128]{1,0:T(8,128)S(1)}, f32[272,128]{1,0:T(8,128)S(1)}, u32[]{:S(2)}, u32[]{:S(2)}) collective-permute-start(f32[272,128]{1,0:T(8,128)S(1)} %shard_map.51.refs_1_.refs_0_), channel_id=1, source_target_pairs={{0,4},{2,6},{4,0},{6,2},{8,12},{10,14},{12,8},{14,10},{1,5},{3,7},... | collective-permute-start | bytes 417800 | tf_op jit(solution)/shard_map/ppermute | solution.py:23
  36.3 28.8 %collective-permute-start.8 = (f32[384,128]{1,0:T(8,128)S(1)}, f32[384,128]{1,0:T(8,128)S(1)}, u32[]{:S(2)}, u32[]{:S(2)}) collective-permute-start(f32[384,128]{1,0:T(8,128)S(1)} %shard_map.52.refs_0_.refs_1_), channel_id=1, source_target_pairs={{0,8},{2,10},{4,12},{6,14},{8,0},{10,2},{12,4},{14,6},{1,9},{3,11}... | collective-permute-start | bytes 589832 | tf_op jit(solution)/shard_map/ppermute | solution.py:23
  39.7 29.7 %collective-permute-start.7 = (f32[384,128]{1,0:T(8,128)S(1)}, f32[384,128]{1,0:T(8,128)S(1)}, u32[]{:S(2)}, u32[]{:S(2)}) collective-permute-start(f32[384,128]{1,0:T(8,128)S(1)} %shard_map.50.refs_0_), channel_id=1, source_target_pairs={{0,8},{2,10},{4,12},{6,14},{8,0},{10,2},{12,4},{14,6},{1,9},{3,11}... | collective-permute-start | bytes 589832 | tf_op jit(solution)/shard_map/ppermute | solution.py:23
  41.0 20.5 %collective-permute-start.9 = (f32[272,128]{1,0:T(8,128)S(1)}, f32[272,128]{1,0:T(8,128)S(1)}, u32[]{:S(2)}, u32[]{:S(2)}) collective-permute-start(f32[272,128]{1,0:T(8,128)S(1)} %shard_map.53.refs_0_.refs_1_), channel_id=1, source_target_pairs={{0,8},{2,10},{4,12},{6,14},{8,0},{10,2},{12,4},{14,6},{1,9},{3,11}... | collective-permute-start | bytes 417800 | tf_op jit(solution)/shard_map/ppermute | solution.py:23

commit v2 on v1

--- a/solution.py
+++ b/solution.py
@@ -63,7 +63,7 @@
         return self.channels * (self.count(c) + (self.ext[level] if c == 0 else 0))
 
 
-def stats_kernel(plan, x_ref, widths_ref, msg_ref, caps_ref):
+def stats_kernel(plan, x_ref, msg_ref):
     ch, rows = plan.channels, plan.rows
     for group in range(ch // 8):
         base = group * rows * 8
@@ -85,15 +85,15 @@
         msg_ref[pl.ds(ch + 8 * group, 8), :] = jnp.broadcast_to(spread, (8, LANES))
         for i in range(plan.lead):
             msg_ref[pl.ds(2 * ch + (group * plan.lead + i) * 8, 8), :] = x_ref[pl.ds(base + 8 * i, 8), :]
+
+
+def local_kernel(plan, stride, x_ref, mine_ref, other_ref, delays_ref, widths_ref, *rest):
+    outs, (caps_ref, stat, first, second) = rest[: len(plan.chunks)], rest[len(plan.chunks) :]
     width = lax.broadcasted_iota(jnp.int32, (WMAX, LANES), 0) + 1
     caps = jnp.full((WMAX, LANES), -jnp.inf, jnp.float32)
     for k in range(widths_ref.shape[0]):
         caps = jnp.where(width == widths_ref[k], jnp.inf, caps)
     caps_ref[...] = caps
-
-
-def local_kernel(plan, stride, x_ref, mine_ref, other_ref, delays_ref, *rest):
-    outs, (stat, first, second) = rest[: len(plan.chunks)], rest[len(plan.chunks) :]
     ch, rows, lead = plan.channels, plan.rows, plan.lead
     half = rows * LANES
     mean_a, mean_b = mine_ref[pl.ds(0, ch), :], other_ref[pl.ds(0, ch), :]
@@ -177,10 +177,10 @@
 
 def merge_kernel(plan, c, level, stride, *refs):
     if c == 0:
-        own_ref, got_ref, delays_ref, out_ref, both = refs
+        own_ref, got_ref, delays_ref, _, out_ref, both = refs
         own_next = got_next = None
     else:
-        own_ref, own_next, got_ref, got_next, delays_ref, out_ref, both = refs
+        own_ref, own_next, got_ref, got_next, delays_ref, _, out_ref, both = refs
     n = plan.count(c)
     gather_rows(plan, c, level, stride, both, own_ref, own_next, got_ref, got_next)
     upper = lax.axis_index("freq") // 2**level % 2 == 1
@@ -194,14 +194,41 @@
             put(plan, outs, level + 1, r, k + plan.chunks[c][0] // 8, tile)
 
 
+def boxcars(count, n, pitch, scale, series, caps_ref, box, lane):
+    tiles = n // 8
+    together = max(d for d in (1, 2, 4, 8) if d * tiles <= 8 or d == 1)
+
+    def some_rows(step, carry):
+        places = [(step * together + i, k) for i in range(together) for k in range(tiles)]
+        here = [series[pl.ds(r * pitch + 8 * k, 8), :] for r, k in places]
+        after = [series[pl.ds(r * pitch + 8 * k + 1, 8), :] for r, k in places]
+        running = here
+        best = None
+        for offset in range(WMAX):
+            if offset:
+                running = [
+                    total + pltpu.roll(jnp.where(lane >= offset, a, b), LANES - offset, 1)
+                    for total, a, b in zip(running, here, after)
+                ]
+            cap = jnp.broadcast_to(caps_ref[pl.ds(offset, 1), :], (8, LANES))
+            factor = scale / math.sqrt(offset + 1)
+            value = [jnp.minimum(total * factor, cap) for total in running]
+            best = value if best is None else [jnp.maximum(a, b) for a, b in zip(best, value)]
+        for (r, k), tile in zip(places, best):
+            box[pl.ds((r // 8) * (n * 8) + 64 * k + r % 8, 8, stride=8), :] = tile
+        return carry
+
+    lax.fori_loop(0, count // together, some_rows, 0)
+
+
 def final_kernel(plan, c, stride, *refs):
     level = plan.levels - 1
     ch, n = plan.channels, plan.count(c)
     if c == 0:
-        own_ref, got_ref, delays_ref, caps_ref, out_ref, head_ref, both, series, box, sem = refs
+        own_ref, got_ref, delays_ref, caps_ref, _, out_ref, head_ref, both, series, box, sem = refs
         own_next = got_next = None
     else:
-        (own_ref, own_next, got_ref, got_next, after_ref, delays_ref, caps_ref, _, out_ref, head_ref,
+        (own_ref, own_next, got_ref, got_next, after_ref, delays_ref, caps_ref, _, _, out_ref, head_ref,
          both, series, box, sem) = refs
     gather_rows(plan, c, level, stride, both, own_ref, own_next, got_ref, got_next)
     upper = lax.axis_index("freq") // 2**level % 2 == 1
@@ -218,27 +245,7 @@
         if c > 0:
             series[pl.ds(r * pitch + n, 1), :] = after_ref[pl.ds(r, 1), :]
 
-    def one_row(r, carry):
-        at = pl.multiple_of(r * pitch, 8)
-        here = [series[pl.ds(at + 8 * k, 8), :] for k in range(tiles)]
-        after = [series[pl.ds(at + 8 * k + 1, 8), :] for k in range(tiles)]
-        running = here
-        best = None
-        for offset in range(WMAX):
-            if offset:
-                running = [
-                    total + pltpu.roll(jnp.where(lane >= offset, a, b), LANES - offset, 1)
-                    for total, a, b in zip(running, here, after)
-                ]
-            cap = jnp.broadcast_to(caps_ref[pl.ds(offset, 1), :], (8, LANES))
-            factor = scale / math.sqrt(offset + 1)
-            value = [jnp.minimum(total * factor, cap) for total in running]
-            best = value if best is None else [jnp.maximum(a, b) for a, b in zip(best, value)]
-        for k in range(tiles):
-            box[pl.ds((r // 8) * (n * 8) + 64 * k + r % 8, 8, stride=8), :] = best[k]
-        return carry
-
-    lax.fori_loop(0, ch, one_row, 0)
+    boxcars(ch, n, pitch, scale, series, caps_ref, box, lane)
     start = plan.chunks[c][0]
     copies = [
         pltpu.make_async_copy(
@@ -263,8 +270,7 @@
     return jax.ShapeDtypeStruct(shape, jnp.float32)
 
 
-def call(kernel, ins, specs, outs, out_specs, scratch, ops, aliases=None):
-    size = sum(math.prod(o.shape) for o in outs) * 4
+def call(kernel, ins, specs, outs, out_specs, scratch, aliases=None):
     return pl.pallas_call(
         kernel,
         in_specs=specs,
@@ -272,7 +278,7 @@
         out_specs=out_specs,
         scratch_shapes=scratch,
         input_output_aliases=aliases or {},
-        cost_estimate=pl.CostEstimate(flops=ops, bytes_accessed=3 * size, transcendentals=0),
+        cost_estimate=pl.CostEstimate(flops=1, bytes_accessed=1, transcendentals=0),
         compiler_params=pltpu.CompilerParams(vmem_limit_bytes=24 * 2**20),
     )(*ins)
 
@@ -281,44 +287,47 @@
     ch, rows = plan.channels, plan.rows
     chunks = range(len(plan.chunks))
     x = spectra.reshape(ch // 8, 8, rows, LANES).transpose(0, 2, 1, 3).reshape(ch * rows, LANES)
-    msg, caps = call(
-        functools.partial(stats_kernel, plan), (x, widths), [VMEM, SMEM],
-        [f32(2 * ch + ch * plan.lead, LANES), f32(WMAX, LANES)], [VMEM, VMEM], [], 10**6,
+    (msg,) = call(
+        functools.partial(stats_kernel, plan), (x,), [VMEM], [f32(2 * ch + ch * plan.lead, LANES)], [VMEM], [],
     )
     other = swap(msg, "tm", 1)
     stride = rows + up(plan.lead, 8) + 8
-    held = call(
-        functools.partial(local_kernel, plan, stride), (x, msg, other, local_delays),
-        [VMEM, VMEM, VMEM, SMEM], [f32(plan.message_rows(c, 0), LANES) for c in chunks],
-        [VMEM for _ in chunks],
+    *first, caps = call(
+        functools.partial(local_kernel, plan, stride), (x, msg, other, local_delays, widths),
+        [VMEM, VMEM, VMEM, SMEM, SMEM], [*(f32(plan.message_rows(c, 0), LANES) for c in chunks), f32(WMAX, LANES)],
+        [VMEM for _ in range(len(chunks) + 1)],
         [pltpu.VMEM((2 * ch, LANES), jnp.float32)] + [pltpu.VMEM((ch * stride, LANES), jnp.float32)] * 2,
-        4 * 10**6,
     )
-    for level in range(plan.levels):
-        got = [swap(held[c], "freq", 2**level) for c in chunks]
-        span = ch * 2**level
-        made = []
-        for c in chunks:
+    held, got = {}, {}
+    for c in chunks:
+        held[0, c] = first[c]
+        got[0, c] = swap(first[c], "freq", 1)
+    last, head, result = caps, None, None
+    for wave in range(len(chunks) + plan.levels - 1):
+        for level in range(plan.levels):
+            c = wave - level
+            if c not in chunks:
+                continue
             n = plan.count(c)
-            tail = max(up(plan.ext[level + 1], 8) if c == 0 else 0, 0) + span // LANES + 1
-            tail = max(tail, plan.ext[level], up(span // LANES + 1, 8))
+            span = ch * 2**level
+            ahead = span // LANES + 1
+            tail = max((up(plan.ext[level + 1], 8) if c == 0 else 0) + ahead, plan.ext[level], up(ahead, 8))
             stride = up(n + tail, 8)
             both = pltpu.VMEM((2 * ch * stride, LANES), jnp.float32)
-            if c == 0:
-                ins, specs = [held[0], got[0]], [VMEM] * 2
-            else:
-                ins, specs = [held[c], held[c - 1], got[c], got[c - 1]], [VMEM] * 4
+            near = [c] if c == 0 else [c, c - 1]
+            ins = [group[level, i] for group in (held, got) for i in near]
+            specs = [VMEM] * len(ins)
             if level < plan.levels - 1:
-                (out,) = call(
-                    functools.partial(merge_kernel, plan, c, level, stride), (*ins, merge_delays),
-                    [*specs, SMEM], [f32(plan.message_rows(c, level + 1), LANES)], [VMEM], [both],
-                    8 * ch * n * LANES,
+                (last,) = call(
+                    functools.partial(merge_kernel, plan, c, level, stride), (*ins, merge_delays, last),
+                    [*specs, SMEM, ANY], [f32(plan.message_rows(c, level + 1), LANES)], [VMEM], [both],
                 )
-                made.append(out)
+                held[level + 1, c] = last
+                got[level + 1, c] = swap(last, "freq", 2 ** (level + 1))
                 continue
             if c > 0:
                 ins, specs = [*ins, head], [*specs, VMEM]
-            ins, specs = [*ins, merge_delays, caps], [*specs, SMEM, VMEM]
+            ins, specs = [*ins, merge_delays, caps, last], [*specs, SMEM, VMEM, ANY]
             aliases = {}
             if c > 0:
                 aliases = {len(ins): 0}
@@ -327,10 +336,9 @@
                 functools.partial(final_kernel, plan, c, stride), ins, specs,
                 [f32(ch * rows, LANES), f32(ch, LANES)], [ANY, VMEM],
                 [both, pltpu.VMEM((ch * (n + 8), LANES), jnp.float32),
-                 pltpu.VMEM((ch * n, LANES), jnp.float32), pltpu.SemaphoreType.DMA((ch // 8,))],
-                200 * ch * n * LANES, aliases,
+                 pltpu.VMEM((ch * n, LANES), jnp.float32), pltpu.SemaphoreType.DMA((ch // 8,))], aliases,
             )
-        held = made
+            last = head
     return result.reshape(ch // 8, rows, 8, LANES).transpose(0, 2, 1, 3).reshape(ch, rows * LANES)
 
 

time: 74.5 us -> 52.7 us (0.71)
  waiting for transfers between devices: 37.4 us -> 15.3 us
  starting transfers between devices: 15.1 us -> 18.7 us
  Pallas kernels: 20 us -> 17.4 us
    ppermute x10, waiting for transfers between devices: 37.4 us -> 15.3 us  [swap(): return lax.ppermute(value, axis, pairs)]
    ppermute x10, starting transfers between devices: 15.1 us -> 18.7 us  [swap(): return lax.ppermute(value, axis, pairs)]
    pallas_call x11, Pallas kernels: 20 us -> 17.4 us  [call(): pl.pallas_call(kernel, in_specs=specs, out_shape=outs, out_specs=out_spec...]
  transfers between devices with their start and end apart: 10 -> 10, of which waited for: 4 -> 6; matrix products, arithmetic and copies ran while one was open for 0% -> 0% of each run, Pallas kernels for 17% -> 21%
where the time goes in v2:
time: 52.7 us; the launch traced here: 52.5 us
  starting transfers between devices  18.7 us (35%)
  Pallas kernels  17.4 us (33%)
  waiting for transfers between devices  15.3 us (29%)
  local copies, waits for them, and re-layouts  1.06 us (2%)
    ppermute x10, starting transfers between devices, swap(): return lax.ppermute(value, axis, pairs)  18.7 us
    pallas_call x11, Pallas kernels, call(): pl.pallas_call(kernel, in_specs=specs, out_shape=outs, out_specs=out_spec...  17.4 us
    ppermute x10, waiting for transfers between devices, swap(): return lax.ppermute(value, axis, pairs)  15.3 us
    unnamed x9, local copies, waits for them, and re-layouts  1.06 us
  transfers between devices with their start and end apart: 10, of which 6 were waited for; matrix products, arithmetic and copies ran while one was open for 0% of the time, Pallas kernels for 21%

profile of v2, /device:TPU:0, one launch (start us, length us, event | category | flops | bytes accessed | tf_op | source)
XLA Modules:
  0.0 52.5 jit_solution(6984533541966009176)
XLA Ops:
  0.0 0.0 copy-start
  0.0 1.0 %copy-done = f32[16,8192]{1,0:T(8,128)S(1)} copy-done((f32[16,8192]{1,0:T(8,128)S(1)}, f32[16,8192]{1,0:T(8,128)}, u32[]{:S(2)}) %copy-start) | copy-done | bytes 524312
  1.0 0.0 copy-start.3
  1.0 0.2 shard_map.46.mine_ref
  1.3 0.0 copy-start.2
  1.3 0.5 collective-permute-start
  1.7 0.0 copy-done.3
  1.7 0.9 %collective-permute-done.other_ref = f32[64,128]{1,0:T(8,128)S(1)} collective-permute-done((f32[64,128]{1,0:T(8,128)S(1)}, f32[64,128]{1,0:T(8,128)S(1)}, u32[]{:S(2)}, u32[]{:S(2)}) %collective-permute-start) | collective-permute-done | bytes 32800 | tf_op jit(solution)/shard_map/ppermute | solution.py:23
  2.6 0.0 copy-done.2
  2.6 1.7 %shard_map.47 = (f32[288,128]{1,0:T(8,128)S(1)}, f32[384,128]{1,0:T(8,128)S(1)}, f32[384,128]{1,0:T(8,128)S(1)}, f32[32,128]{1,0:T(8,128)S(1)}) custom-call(f32[1024,128]{1,0:T(8,128)S(1)} %bitcast.11, f32[64,128]{1,0:T(8,128)S(1)} %shard_map.46.mine_ref, f32[64,128]{1,0:T(8,128)S(1)} %collective-permute-done.other_ref, s32[4,3,16]{2,1,0:T(4,128)S(1)} %copy.7.delays_ref, ...), custom_call_target="tpu_custom_call" | custom-call | flops 1 | bytes 1 | tf_op jit(solution)/shard_map/pallas_call | solution.py:274
  4.3 0.0 copy-start.1
  4.3 2.9 %collective-permute-start.3 = (f32[288,128]{1,0:T(8,128)S(1)}, f32[288,128]{1,0:T(8,128)S(1)}, u32[]{:S(2)}, u32[]{:S(2)}) collective-permute-start(f32[288,128]{1,0:T(8,128)S(1)} %get-tuple-element.16.refs_0_.refs_1_), channel_id=1, source_target_pairs={{0,2},{2,0},{4,6},{6,4},{8,10},{10,8},{12,14},{14,12},{1,3},{3,1},... | collective-permute-start | bytes 442376 | tf_op jit(solution)/shard_map/ppermute | solution.py:23
  7.2 0.1 collective-permute-start.2
  7.3 1.9 %collective-permute-start.1 = (f32[384,128]{1,0:T(8,128)S(1)}, f32[384,128]{1,0:T(8,128)S(1)}, u32[]{:S(2)}, u32[]{:S(2)}) collective-permute-start(f32[384,128]{1,0:T(8,128)S(1)} %get-tuple-element.14.refs_0_), channel_id=1, source_target_pairs={{0,2},{2,0},{4,6},{6,4},{8,10},{10,8},{12,14},{14,12},{1,3},{3,1},... | collective-permute-start | bytes 589832 | tf_op jit(solution)/shard_map/ppermute | solution.py:23
  9.2 2.6 %collective-permute-done.3.refs_1_.refs_3_ = f32[288,128]{1,0:T(8,128)S(1)} collective-permute-done((f32[288,128]{1,0:T(8,128)S(1)}, f32[288,128]{1,0:T(8,128)S(1)}, u32[]{:S(2)}, u32[]{:S(2)}) %collective-permute-start.3) | collective-permute-done | bytes 147488 | tf_op jit(solution)/shard_map/ppermute | solution.py:23
  11.8 0.0 copy-done.1
  11.8 0.8 %shard_map.48.refs_5_.refs_0_.refs_1_ = f32[272,128]{1,0:T(8,128)S(1)} custom-call(f32[288,128]{1,0:T(8,128)S(1)} %get-tuple-element.16.refs_0_.refs_1_, f32[288,128]{1,0:T(8,128)S(1)} %collective-permute-done.3.refs_1_.refs_3_, s32[3,3,16]{2,1,0:T(4,128)S(1)} %copy-done.1, f32[32,128]{1,0:T(8,128)S(1)} %get-tuple-element.17.refs_3_.refs_6_), custom_call_target="tpu_custom_call" | custom-call | flops 1 | bytes 1 | tf_op jit(solution)/shard_map/pallas_call | solution.py:274
  12.7 2.2 %collective-permute-start.4 = (f32[272,128]{1,0:T(8,128)S(1)}, f32[272,128]{1,0:T(8,128)S(1)}, u32[]{:S(2)}, u32[]{:S(2)}) collective-permute-start(f32[272,128]{1,0:T(8,128)S(1)} %shard_map.48.refs_5_.refs_0_.refs_1_), channel_id=1, source_target_pairs={{0,4},{2,6},{4,0},{6,2},{8,12},{10,14},{12,8},{14,10},{1,5},{3,7},... | collective-permute-start | bytes 417800 | tf_op jit(solution)/shard_map/ppermute | solution.py:23
  14.9 1.2 %collective-permute-done.2.refs_2_.refs_3_ = f32[384,128]{1,0:T(8,128)S(1)} collective-permute-done((f32[384,128]{1,0:T(8,128)S(1)}, f32[384,128]{1,0:T(8,128)S(1)}, u32[]{:S(2)}, u32[]{:S(2)}) %collective-permute-start.2) | collective-permute-done | bytes 196640 | tf_op jit(solution)/shard_map/ppermute | solution.py:23
  16.1 0.8 %shard_map.49.refs_3_.refs_0_.refs_1_ = f32[384,128]{1,0:T(8,128)S(1)} custom-call(f32[384,128]{1,0:T(8,128)S(1)} %get-tuple-element.15.refs_0_.refs_1_, f32[288,128]{1,0:T(8,128)S(1)} %get-tuple-element.16.refs_0_.refs_1_, f32[384,128]{1,0:T(8,128)S(1)} %collective-permute-done.2.refs_2_.refs_3_, f32[288,128]{1,0:T(8,128)S(1)} %collective-permute-done.3.refs_1_.refs_3_, ...), custom_call_target="tpu_custom_call" | custom-call | flops 1 | bytes 1 | tf_op jit(solution)/shard_map/pallas_call | solution.py:274
  16.9 2.2 %collective-permute-start.6 = (f32[384,128]{1,0:T(8,128)S(1)}, f32[384,128]{1,0:T(8,128)S(1)}, u32[]{:S(2)}, u32[]{:S(2)}) collective-permute-start(f32[384,128]{1,0:T(8,128)S(1)} %shard_map.49.refs_3_.refs_0_.refs_1_), channel_id=1, source_target_pairs={{0,4},{2,6},{4,0},{6,2},{8,12},{10,14},{12,8},{14,10},{1,5},{3,7},... | collective-permute-start | bytes 589832 | tf_op jit(solution)/shard_map/ppermute | solution.py:23
  19.1 0.0 collective-permute-done.4.refs_1_.refs_3_
  19.1 0.8 %shard_map.50.refs_5_.refs_0_.refs_1_ = f32[272,128]{1,0:T(8,128)S(1)} custom-call(f32[272,128]{1,0:T(8,128)S(1)} %shard_map.48.refs_5_.refs_0_.refs_1_, f32[272,128]{1,0:T(8,128)S(1)} %collective-permute-done.4.refs_1_.refs_3_, s32[3,3,16]{2,1,0:T(4,128)S(1)} %copy-done.1, f32[384,128]{1,0:T(8,128)S(1)} %shard_map.49.refs_3_.refs_0_.refs_1_), custom_call_target="tpu_custom_call" | custom-call | flops 1 | bytes 1 | tf_op jit(solution)/shard_map/pallas_call | solution.py:274
  19.9 0.0 collective-permute-done.1.refs_2_
  19.9 0.8 %shard_map.51.refs_5_.refs_0_ = f32[384,128]{1,0:T(8,128)S(1)} custom-call(f32[384,128]{1,0:T(8,128)S(1)} %get-tuple-element.14.refs_0_, f32[384,128]{1,0:T(8,128)S(1)} %get-tuple-element.15.refs_0_.refs_1_, f32[384,128]{1,0:T(8,128)S(1)} %collective-permute-done.1.refs_2_, f32[384,128]{1,0:T(8,128)S(1)} %collective-permute-done.2.refs_2_.refs_3_, ...), custom_call_target="tpu_custom_call" | custom-call | flops 1 | bytes 1 | tf_op jit(solution)/shard_map/pallas_call | solution.py:274
  20.7 1.8 %collective-permute-start.5 = (f32[384,128]{1,0:T(8,128)S(1)}, f32[384,128]{1,0:T(8,128)S(1)}, u32[]{:S(2)}, u32[]{:S(2)}) collective-permute-start(f32[384,128]{1,0:T(8,128)S(1)} %shard_map.51.refs_5_.refs_0_), channel_id=1, source_target_pairs={{0,4},{2,6},{4,0},{6,2},{8,12},{10,14},{12,8},{14,10},{1,5},{3,7},... | collective-permute-start | bytes 589832 | tf_op jit(solution)/shard_map/ppermute | solution.py:23
  22.5 2.6 %collective-permute-start.7 = (f32[272,128]{1,0:T(8,128)S(1)}, f32[272,128]{1,0:T(8,128)S(1)}, u32[]{:S(2)}, u32[]{:S(2)}) collective-permute-start(f32[272,128]{1,0:T(8,128)S(1)} %shard_map.50.refs_5_.refs_0_.refs_1_), channel_id=1, source_target_pairs={{0,8},{2,10},{4,12},{6,14},{8,0},{10,2},{12,4},{14,6},{1,9},{3,11}... | collective-permute-start | bytes 417800 | tf_op jit(solution)/shard_map/ppermute | solution.py:23
  25.1 0.0 collective-permute-done.6.refs_2_.refs_3_
  25.1 0.8 %shard_map.52.refs_4_.refs_0_.refs_1_ = f32[384,128]{1,0:T(8,128)S(1)} custom-call(f32[384,128]{1,0:T(8,128)S(1)} %shard_map.49.refs_3_.refs_0_.refs_1_, f32[272,128]{1,0:T(8,128)S(1)} %shard_map.48.refs_5_.refs_0_.refs_1_, f32[384,128]{1,0:T(8,128)S(1)} %collective-permute-done.6.refs_2_.refs_3_, f32[272,128]{1,0:T(8,128)S(1)} %collective-permute-done.4.refs_1_.refs_3_, ...), custom_call_target="tpu_custom_call" | custom-call | flops 1 | bytes 1 | tf_op jit(solution)/shard_map/pallas_call | solution.py:274
  25.9 1.0 %collective-permute-start.9 = (f32[384,128]{1,0:T(8,128)S(1)}, f32[384,128]{1,0:T(8,128)S(1)}, u32[]{:S(2)}, u32[]{:S(2)}) collective-permute-start(f32[384,128]{1,0:T(8,128)S(1)} %shard_map.52.refs_4_.refs_0_.refs_1_), channel_id=1, source_target_pairs={{0,8},{2,10},{4,12},{6,14},{8,0},{10,2},{12,4},{14,6},{1,9},{3,11}... | collective-permute-start | bytes 589832 | tf_op jit(solution)/shard_map/ppermute | solution.py:23
  26.9 4.0 %collective-permute-done.7.refs_1_.refs_3_ = f32[272,128]{1,0:T(8,128)S(1)} collective-permute-done((f32[272,128]{1,0:T(8,128)S(1)}, f32[272,128]{1,0:T(8,128)S(1)}, u32[]{:S(2)}, u32[]{:S(2)}) %collective-permute-start.7) | collective-permute-done | bytes 139296 | tf_op jit(solution)/shard_map/ppermute | solution.py:23
  30.9 2.8 %shard_map.53 = (f32[1024,128]{1,0:T(8,128)}, f32[16,128]{1,0:T(8,128)S(1)}) custom-call(f32[272,128]{1,0:T(8,128)S(1)} %shard_map.50.refs_5_.refs_0_.refs_1_, f32[272,128]{1,0:T(8,128)S(1)} %collective-permute-done.7.refs_1_.refs_3_, s32[3,3,16]{2,1,0:T(4,128)S(1)} %copy-done.1, f32[32,128]{1,0:T(8,128)S(1)} %get-tuple-element.17.refs_3_.refs_6_, ...), custom_call_target="tpu_custom_call" | custom-call | flops 1 | bytes 1 | tf_op jit(solution)/shard_map/pallas_call | solution.py:274
  33.7 0.0 collective-permute-done.5.refs_2_
  33.7 0.8 %shard_map.54.refs_7_.refs_0_ = f32[384,128]{1,0:T(8,128)S(1)} custom-call(f32[384,128]{1,0:T(8,128)S(1)} %shard_map.51.refs_5_.refs_0_, f32[384,128]{1,0:T(8,128)S(1)} %shard_map.49.refs_3_.refs_0_.refs_1_, f32[384,128]{1,0:T(8,128)S(1)} %collective-permute-done.5.refs_2_, f32[384,128]{1,0:T(8,128)S(1)} %collective-permute-done.6.refs_2_.refs_3_, ...), custom_call_target="tpu_custom_call" | custom-call | flops 1 | bytes 1 | tf_op jit(solution)/shard_map/pallas_call | solution.py:274
  34.5 3.5 %collective-permute-start.8 = (f32[384,128]{1,0:T(8,128)S(1)}, f32[384,128]{1,0:T(8,128)S(1)}, u32[]{:S(2)}, u32[]{:S(2)}) collective-permute-start(f32[384,128]{1,0:T(8,128)S(1)} %shard_map.54.refs_7_.refs_0_), channel_id=1, source_target_pairs={{0,8},{2,10},{4,12},{6,14},{8,0},{10,2},{12,4},{14,6},{1,9},{3,11}... | collective-permute-start | bytes 589832 | tf_op jit(solution)/shard_map/ppermute | solution.py:23
  38.0 4.8 %collective-permute-done.9.refs_2_.refs_3_ = f32[384,128]{1,0:T(8,128)S(1)} collective-permute-done((f32[384,128]{1,0:T(8,128)S(1)}, f32[384,128]{1,0:T(8,128)S(1)}, u32[]{:S(2)}, u32[]{:S(2)}) %collective-permute-start.9) | collective-permute-done | bytes 196640 | tf_op jit(solution)/shard_map/ppermute | solution.py:23
  42.8 3.6 %shard_map.55 = (f32[1024,128]{1,0:T(8,128)}, f32[16,128]{1,0:T(8,128)S(1)}) custom-call(f32[384,128]{1,0:T(8,128)S(1)} %shard_map.52.refs_4_.refs_0_.refs_1_, f32[272,128]{1,0:T(8,128)S(1)} %shard_map.50.refs_5_.refs_0_.refs_1_, f32[384,128]{1,0:T(8,128)S(1)} %collective-permute-done.9.refs_2_.refs_3_, ...), custom_call_target="tpu_custom_call", output_to_operand_aliasing={{0}: (8, {})} | custom-call | flops 1 | bytes 1 | tf_op jit(solution)/shard_map/pallas_call | solution.py:274
  46.4 1.9 %collective-permute-done.8.refs_2_ = f32[384,128]{1,0:T(8,128)S(1)} collective-permute-done((f32[384,128]{1,0:T(8,128)S(1)}, f32[384,128]{1,0:T(8,128)S(1)}, u32[]{:S(2)}, u32[]{:S(2)}) %collective-permute-start.8) | collective-permute-done | bytes 196640 | tf_op jit(solution)/shard_map/ppermute | solution.py:23
  48.3 4.2 %shard_map.56 = (f32[1024,128]{1,0:T(8,128)}, f32[16,128]{1,0:T(8,128)}) custom-call(f32[384,128]{1,0:T(8,128)S(1)} %shard_map.54.refs_7_.refs_0_, f32[384,128]{1,0:T(8,128)S(1)} %shard_map.52.refs_4_.refs_0_.refs_1_, f32[384,128]{1,0:T(8,128)S(1)} %collective-permute-done.8.refs_2_, ...), custom_call_target="tpu_custom_call", output_to_operand_aliasing={{0}: (8, {})} | custom-call | flops 1 | bytes 1 | tf_op jit(solution)/shard_map/pallas_call | solution.py:274
  (1 shorter events, 0.0 us)
Async XLA Ops:
  0.0 1.0 %copy-start = (f32[16,8192]{1,0:T(8,128)S(1)}, f32[16,8192]{1,0:T(8,128)}, u32[]{:S(2)}) copy-start(f32[16,8192]{1,0:T(8,128)} %param.4) | copy-start | bytes 1572868
  1.0 0.7 %copy-start.3 = (s32[4,3,16]{2,0,1:T(4,128)S(1)}, s32[4,3,16]{2,0,1:T(4,128)}, u32[]{:S(2)}) copy-start(s32[4,3,16]{2,0,1:T(4,128)} %param.5) | copy-start | bytes 2308
  1.3 1.3 %copy-start.2 = (s32[16]{0:T(128)S(1)}, s32[16]{0:T(128)}, u32[]{:S(2)}) copy-start(s32[16]{0:T(128)} %widths_ref.1) | copy-start | bytes 196
  1.3 1.3 %collective-permute-start = (f32[64,128]{1,0:T(8,128)S(1)}, f32[64,128]{1,0:T(8,128)S(1)}, u32[]{:S(2)}, u32[]{:S(2)}) collective-permute-start(f32[64,128]{1,0:T(8,128)S(1)} %shard_map.46.mine_ref), channel_id=1, source_target_pairs={{0,1},{1,0},{2,3},{3,2},{4,5},{5,4},{6,7},{7,6},{8,9},{9,8},{10,11... | collective-permute-start | bytes 98312 | tf_op jit(solution)/shard_map/ppermute | solution.py:23
  4.3 7.5 %copy-start.1 = (s32[3,3,16]{2,1,0:T(4,128)S(1)}, s32[3,3,16]{2,1,0:T(4,128)}, u32[]{:S(2)}) copy-start(s32[3,3,16]{2,1,0:T(4,128)} %refs_5_.3) | copy-start | bytes 1732
  4.3 7.5 %collective-permute-start.3 = (f32[288,128]{1,0:T(8,128)S(1)}, f32[288,128]{1,0:T(8,128)S(1)}, u32[]{:S(2)}, u32[]{:S(2)}) collective-permute-start(f32[288,128]{1,0:T(8,128)S(1)} %get-tuple-element.16.refs_0_.refs_1_), channel_id=1, source_target_pairs={{0,2},{2,0},{4,6},{6,4},{8,10},{10,8},{12,14},{14,12},{1,3},{3,1},... | collective-permute-start | bytes 442376 | tf_op jit(solution)/shard_map/ppermute | solution.py:23
  7.2 8.8 %collective-permute-start.2 = (f32[384,128]{1,0:T(8,128)S(1)}, f32[384,128]{1,0:T(8,128)S(1)}, u32[]{:S(2)}, u32[]{:S(2)}) collective-permute-start(f32[384,128]{1,0:T(8,128)S(1)} %get-tuple-element.15.refs_0_.refs_1_), channel_id=1, source_target_pairs={{0,2},{2,0},{4,6},{6,4},{8,10},{10,8},{12,14},{14,12},{1,3},{3,1},... | collective-permute-start | bytes 589832 | tf_op jit(solution)/shard_map/ppermute | solution.py:23
  7.3 12.6 %collective-permute-start.1 = (f32[384,128]{1,0:T(8,128)S(1)}, f32[384,128]{1,0:T(8,128)S(1)}, u32[]{:S(2)}, u32[]{:S(2)}) collective-permute-start(f32[384,128]{1,0:T(8,128)S(1)} %get-tuple-element.14.refs_0_), channel_id=1, source_target_pairs={{0,2},{2,0},{4,6},{6,4},{8,10},{10,8},{12,14},{14,12},{1,3},{3,1},... | collective-permute-start | bytes 589832 | tf_op jit(solution)/shard_map/ppermute | solution.py:23
  12.7 6.4 %collective-permute-start.4 = (f32[272,128]{1,0:T(8,128)S(1)}, f32[272,128]{1,0:T(8,128)S(1)}, u32[]{:S(2)}, u32[]{:S(2)}) collective-permute-start(f32[272,128]{1,0:T(8,128)S(1)} %shard_map.48.refs_5_.refs_0_.refs_1_), channel_id=1, source_target_pairs={{0,4},{2,6},{4,0},{6,2},{8,12},{10,14},{12,8},{14,10},{1,5},{3,7},... | collective-permute-start | bytes 417800 | tf_op jit(solution)/shard_map/ppermute | solution.py:23
  16.9 8.2 %collective-permute-start.6 = (f32[384,128]{1,0:T(8,128)S(1)}, f32[384,128]{1,0:T(8,128)S(1)}, u32[]{:S(2)}, u32[]{:S(2)}) collective-permute-start(f32[384,128]{1,0:T(8,128)S(1)} %shard_map.49.refs_3_.refs_0_.refs_1_), channel_id=1, source_target_pairs={{0,4},{2,6},{4,0},{6,2},{8,12},{10,14},{12,8},{14,10},{1,5},{3,7},... | collective-permute-start | bytes 589832 | tf_op jit(solution)/shard_map/ppermute | solution.py:23
  20.7 13.0 %collective-permute-start.5 = (f32[384,128]{1,0:T(8,128)S(1)}, f32[384,128]{1,0:T(8,128)S(1)}, u32[]{:S(2)}, u32[]{:S(2)}) collective-permute-start(f32[384,128]{1,0:T(8,128)S(1)} %shard_map.51.refs_5_.refs_0_), channel_id=1, source_target_pairs={{0,4},{2,6},{4,0},{6,2},{8,12},{10,14},{12,8},{14,10},{1,5},{3,7},... | collective-permute-start | bytes 589832 | tf_op jit(solution)/shard_map/ppermute | solution.py:23
  22.5 8.4 %collective-permute-start.7 = (f32[272,128]{1,0:T(8,128)S(1)}, f32[272,128]{1,0:T(8,128)S(1)}, u32[]{:S(2)}, u32[]{:S(2)}) collective-permute-start(f32[272,128]{1,0:T(8,128)S(1)} %shard_map.50.refs_5_.refs_0_.refs_1_), channel_id=1, source_target_pairs={{0,8},{2,10},{4,12},{6,14},{8,0},{10,2},{12,4},{14,6},{1,9},{3,11}... | collective-permute-start | bytes 417800 | tf_op jit(solution)/shard_map/ppermute | solution.py:23
  25.9 16.9 %collective-permute-start.9 = (f32[384,128]{1,0:T(8,128)S(1)}, f32[384,128]{1,0:T(8,128)S(1)}, u32[]{:S(2)}, u32[]{:S(2)}) collective-permute-start(f32[384,128]{1,0:T(8,128)S(1)} %shard_map.52.refs_4_.refs_0_.refs_1_), channel_id=1, source_target_pairs={{0,8},{2,10},{4,12},{6,14},{8,0},{10,2},{12,4},{14,6},{1,9},{3,11}... | collective-permute-start | bytes 589832 | tf_op jit(solution)/shard_map/ppermute | solution.py:23
  34.5 13.8 %collective-permute-start.8 = (f32[384,128]{1,0:T(8,128)S(1)}, f32[384,128]{1,0:T(8,128)S(1)}, u32[]{:S(2)}, u32[]{:S(2)}) collective-permute-start(f32[384,128]{1,0:T(8,128)S(1)} %shard_map.54.refs_7_.refs_0_), channel_id=1, source_target_pairs={{0,8},{2,10},{4,12},{6,14},{8,0},{10,2},{12,4},{14,6},{1,9},{3,11}... | collective-permute-start | bytes 589832 | tf_op jit(solution)/shard_map/ppermute | solution.py:23

commit v3 on v2

--- a/solution.py
+++ b/solution.py
@@ -11,7 +11,7 @@
 WMAX = 32
 LANES = 128
 EPSILON = 1e-05
-SHARES = (2, 3, 3)
+SHARES = (2, 2, 2, 2)
 
 
 def up(value, by):
@@ -34,6 +34,13 @@
 
 def lanes():
     return lax.broadcasted_iota(jnp.int32, (8, LANES), 1)
+
+
+STEP, WAIT = 1.5, 0.0
+
+
+def turn(plan):
+    return lambda job: (job[1] + STEP * job[0] + WAIT * (job[0] == plan.levels - 1), job[0])
 
 
 class Plan:
@@ -121,11 +128,11 @@
         size = 2**level
         final = level == plan.local_levels - 1
         tiles = (rows + up(lead, 8)) // 8
-        for r in range(ch):
+        jobs = table(delays_ref, level, ch)
+        for r, (low, high, delay) in enumerate(jobs):
             base = r // (2 * size) * (2 * size)
-            low = (base + delays_ref[level, 0, r]) * stride
-            high = (base + size + delays_ref[level, 1, r]) * stride
-            delay = delays_ref[level, 2, r]
+            low = (base + low) * stride
+            high = (base + size + high) * stride
             for k in range(tiles):
                 tile = source[pl.ds(pl.multiple_of(low + 8 * k, 8), 8), :] + shifted_tile(
                     source, high + 8 * k, delay, False, lane
@@ -165,13 +172,22 @@
                     both[pl.ds(at + n + 8 * k, 8), :] = following[pl.ds(r * m + 8 * k, 8), :]
 
 
-def merged_tile(plan, level, stride, both, delays_ref, upper, r, k, lane):
+def table(delays_ref, level, count):
+    return [tuple(delays_ref[level, i, r] for i in range(3)) for r in range(count)]
+
+
+def merge_jobs(plan, level, stride, delays_ref):
     ch = plan.channels
-    low = (jnp.where(upper, ch, 0) + delays_ref[level, 0, r]) * stride + 8 * k
-    high = (jnp.where(upper, 0, ch) + delays_ref[level, 1, r]) * stride + 8 * k
-    wide = ch * 2**level >= LANES
-    return both[pl.ds(pl.multiple_of(low, 8), 8), :] + shifted_tile(
-        both, high, delays_ref[level, 2, r], wide, lane
+    upper = lax.axis_index("freq") // 2**level % 2 == 1
+    first, second = jnp.where(upper, ch, 0), jnp.where(upper, 0, ch)
+    return [((first + a) * stride, (second + b) * stride, d) for a, b, d in table(delays_ref, level, ch)]
+
+
+def merged_tile(plan, level, both, job, k, lane):
+    low, high, delay = job
+    wide = plan.channels * 2**level >= LANES
+    return both[pl.ds(pl.multiple_of(low + 8 * k, 8), 8), :] + shifted_tile(
+        both, high + 8 * k, delay, wide, lane
     )
 
 
@@ -182,15 +198,15 @@
     else:
         own_ref, own_next, got_ref, got_next, delays_ref, _, out_ref, both = refs
     n = plan.count(c)
+    jobs = merge_jobs(plan, level, stride, delays_ref)
     gather_rows(plan, c, level, stride, both, own_ref, own_next, got_ref, got_next)
-    upper = lax.axis_index("freq") // 2**level % 2 == 1
     lane = lanes()
     rows = n + (up(plan.ext[level + 1], 8) if c == 0 else 0)
     outs = [None] * len(plan.chunks)
     outs[c] = out_ref
     for r in range(plan.channels):
         for k in range(rows // 8):
-            tile = merged_tile(plan, level, stride, both, delays_ref, upper, r, k, lane)
+            tile = merged_tile(plan, level, both, jobs[r], k, lane)
             put(plan, outs, level + 1, r, k + plan.chunks[c][0] // 8, tile)
 
 
@@ -230,15 +246,15 @@
     else:
         (own_ref, own_next, got_ref, got_next, after_ref, delays_ref, caps_ref, _, _, out_ref, head_ref,
          both, series, box, sem) = refs
+    jobs = merge_jobs(plan, level, stride, delays_ref)
     gather_rows(plan, c, level, stride, both, own_ref, own_next, got_ref, got_next)
-    upper = lax.axis_index("freq") // 2**level % 2 == 1
     lane = lanes()
     tiles = n // 8
     scale = 1.0 / math.sqrt(ch * plan.freq_count)
     pitch = n + 8
     for r in range(ch):
         for k in range(tiles + (1 if c == 0 else 0)):
-            tile = merged_tile(plan, level, stride, both, delays_ref, upper, r, k, lane)
+            tile = merged_tile(plan, level, both, jobs[r], k, lane)
             series[pl.ds(r * pitch + 8 * k, 8), :] = tile
             if k == 0:
                 head_ref[pl.ds(r, 1), :] = tile[:1]
@@ -294,7 +310,7 @@
     stride = rows + up(plan.lead, 8) + 8
     *first, caps = call(
         functools.partial(local_kernel, plan, stride), (x, msg, other, local_delays, widths),
-        [VMEM, VMEM, VMEM, SMEM, SMEM], [*(f32(plan.message_rows(c, 0), LANES) for c in chunks), f32(WMAX, LANES)],
+        [VMEM, VMEM, VMEM, VMEM, VMEM], [*(f32(plan.message_rows(c, 0), LANES) for c in chunks), f32(WMAX, LANES)],
         [VMEM for _ in range(len(chunks) + 1)],
         [pltpu.VMEM((2 * ch, LANES), jnp.float32)] + [pltpu.VMEM((ch * stride, LANES), jnp.float32)] * 2,
     )
@@ -303,11 +319,8 @@
         held[0, c] = first[c]
         got[0, c] = swap(first[c], "freq", 1)
     last, head, result = caps, None, None
-    for wave in range(len(chunks) + plan.levels - 1):
-        for level in range(plan.levels):
-            c = wave - level
-            if c not in chunks:
-                continue
+    for level, c in sorted(((level, c) for level in range(plan.levels) for c in chunks), key=turn(plan)):
+        if True:
             n = plan.count(c)
             span = ch * 2**level
             ahead = span // LANES + 1
@@ -320,14 +333,14 @@
             if level < plan.levels - 1:
                 (last,) = call(
                     functools.partial(merge_kernel, plan, c, level, stride), (*ins, merge_delays, last),
-                    [*specs, SMEM, ANY], [f32(plan.message_rows(c, level + 1), LANES)], [VMEM], [both],
+                    [*specs, VMEM, ANY], [f32(plan.message_rows(c, level + 1), LANES)], [VMEM], [both],
                 )
                 held[level + 1, c] = last
                 got[level + 1, c] = swap(last, "freq", 2 ** (level + 1))
                 continue
             if c > 0:
                 ins, specs = [*ins, head], [*specs, VMEM]
-            ins, specs = [*ins, merge_delays, caps, last], [*specs, SMEM, VMEM, ANY]
+            ins, specs = [*ins, merge_delays, caps, last], [*specs, VMEM, VMEM, ANY]
             aliases = {}
             if c > 0:
                 aliases = {len(ins): 0}

time: 52.7 us -> 47.1 us (0.89)
  the two profiles are of different devices: /device:TPU:0 before, /device:TPU:24 now
where the time goes in v3:
time: 47.1 us; the launch traced here: 46.9 us
  waiting for transfers between devices  22.8 us (48%)
  Pallas kernels  13 us (28%)
  starting transfers between devices  9.49 us (20%)
  local copies, waits for them, and re-layouts  1.5 us (3%)
    ppermute x13, waiting for transfers between devices, swap(): return lax.ppermute(value, axis, pairs)  22.8 us
    pallas_call x14, Pallas kernels, call(): pl.pallas_call(kernel, in_specs=specs, out_shape=outs, out_specs=out_spec...  13 us
    ppermute x13, starting transfers between devices, swap(): return lax.ppermute(value, axis, pairs)  9.49 us
    unnamed x9, local copies, waits for them, and re-layouts  1.5 us
  transfers between devices with their start and end apart: 13, of which 9 were waited for; matrix products, arithmetic and copies ran while one was open for 0% of the time, Pallas kernels for 19%

profile of v3, /device:TPU:24, one launch (start us, length us, event | category | flops | bytes accessed | tf_op | source)
XLA Modules:
  0.0 46.9 jit_solution(17385596609717806189)
XLA Ops:
  0.0 0.0 copy-start
  0.0 1.0 %copy-done = f32[16,8192]{1,0:T(8,128)S(1)} copy-done((f32[16,8192]{1,0:T(8,128)S(1)}, f32[16,8192]{1,0:T(8,128)}, u32[]{:S(2)}) %copy-start) | copy-done | bytes 524312
  1.0 0.0 copy-start.3
  1.0 0.2 shard_map.46.mine_ref
  1.3 0.0 copy-start.2
  1.3 0.0 collective-permute-start
  1.3 0.4 copy-done.3
  1.7 0.7 %collective-permute-done.other_ref = f32[64,128]{1,0:T(8,128)S(1)} collective-permute-done((f32[64,128]{1,0:T(8,128)S(1)}, f32[64,128]{1,0:T(8,128)S(1)}, u32[]{:S(2)}, u32[]{:S(2)}) %collective-permute-start) | collective-permute-done | bytes 32800 | tf_op jit(solution)/shard_map/ppermute | solution.py:23
  2.5 0.0 copy-done.2
  2.5 0.0 copy-start.1
  2.5 1.2 %shard_map.47 = (f32[288,128]{1,0:T(8,128)S(1)}, f32[256,128]{1,0:T(8,128)S(1)}, f32[256,128]{1,0:T(8,128)S(1)}, f32[256,128]{1,0:T(8,128)S(1)}, f32[32,128]{1,0:T(8,128)S(1)}) custom-call(f32[1024,128]{1,0:T(8,128)S(1)} %bitcast.11, f32[64,128]{1,0:T(8,128)S(1)} %shard_map.46.mine_ref, f32[64,128]{1,0:T(8,128)S(1)} %collective-permute-done.other_ref, ...), custom_call_target="tpu_custom_call" | custom-call | flops 1 | bytes 1 | tf_op jit(solution)/shard_map/pallas_call | solution.py:290
  3.7 1.6 %collective-permute-start.4 = (f32[288,128]{1,0:T(8,128)S(1)}, f32[288,128]{1,0:T(8,128)S(1)}, u32[]{:S(2)}, u32[]{:S(2)}) collective-permute-start(f32[288,128]{1,0:T(8,128)S(1)} %get-tuple-element.20.refs_0_.refs_1_), channel_id=1, source_target_pairs={{0,2},{2,0},{4,6},{6,4},{8,10},{10,8},{12,14},{14,12},{1,3},{3,1},... | collective-permute-start | bytes 442376 | tf_op jit(solution)/shard_map/ppermute | solution.py:23
  5.2 0.5 %collective-permute-start.3 = (f32[256,128]{1,0:T(8,128)S(1)}, f32[256,128]{1,0:T(8,128)S(1)}, u32[]{:S(2)}, u32[]{:S(2)}) collective-permute-start(f32[256,128]{1,0:T(8,128)S(1)} %get-tuple-element.19.refs_0_.refs_1_), channel_id=1, source_target_pairs={{0,2},{2,0},{4,6},{6,4},{8,10},{10,8},{12,14},{14,12},{1,3},{3,1},... | collective-permute-start | bytes 393224 | tf_op jit(solution)/shard_map/ppermute | solution.py:23
  5.7 4.7 %collective-permute-done.4.refs_1_.refs_3_ = f32[288,128]{1,0:T(8,128)S(1)} collective-permute-done((f32[288,128]{1,0:T(8,128)S(1)}, f32[288,128]{1,0:T(8,128)S(1)}, u32[]{:S(2)}, u32[]{:S(2)}) %collective-permute-start.4) | collective-permute-done | bytes 147488 | tf_op jit(solution)/shard_map/ppermute | solution.py:23
  10.4 0.0 copy-done.1
  10.4 0.3 shard_map.48.refs_5_.refs_0_.refs_1_
  10.7 0.5 %collective-permute-start.6 = (f32[272,128]{1,0:T(8,128)S(1)}, f32[272,128]{1,0:T(8,128)S(1)}, u32[]{:S(2)}, u32[]{:S(2)}) collective-permute-start(f32[272,128]{1,0:T(8,128)S(1)} %shard_map.48.refs_5_.refs_0_.refs_1_), channel_id=1, source_target_pairs={{0,4},{2,6},{4,0},{6,2},{8,12},{10,14},{12,8},{14,10},{1,5},{3,7},... | collective-permute-start | bytes 417800 | tf_op jit(solution)/shard_map/ppermute | solution.py:23
  11.2 1.5 %collective-permute-start.2 = (f32[256,128]{1,0:T(8,128)S(1)}, f32[256,128]{1,0:T(8,128)S(1)}, u32[]{:S(2)}, u32[]{:S(2)}) collective-permute-start(f32[256,128]{1,0:T(8,128)S(1)} %get-tuple-element.18.refs_0_.refs_1_), channel_id=1, source_target_pairs={{0,2},{2,0},{4,6},{6,4},{8,10},{10,8},{12,14},{14,12},{1,3},{3,1},... | collective-permute-start | bytes 393224 | tf_op jit(solution)/shard_map/ppermute | solution.py:23
  12.7 0.1 collective-permute-done.3.refs_2_.refs_3_
  12.8 0.2 shard_map.49.refs_3_.refs_0_.refs_1_
  13.0 1.5 %collective-permute-start.5 = (f32[256,128]{1,0:T(8,128)S(1)}, f32[256,128]{1,0:T(8,128)S(1)}, u32[]{:S(2)}, u32[]{:S(2)}) collective-permute-start(f32[256,128]{1,0:T(8,128)S(1)} %shard_map.49.refs_3_.refs_0_.refs_1_), channel_id=1, source_target_pairs={{0,4},{2,6},{4,0},{6,2},{8,12},{10,14},{12,8},{14,10},{1,5},{3,7},... | collective-permute-start | bytes 393224 | tf_op jit(solution)/shard_map/ppermute | solution.py:23
  14.6 0.5 %collective-permute-start.1 = (f32[256,128]{1,0:T(8,128)S(1)}, f32[256,128]{1,0:T(8,128)S(1)}, u32[]{:S(2)}, u32[]{:S(2)}) collective-permute-start(f32[256,128]{1,0:T(8,128)S(1)} %get-tuple-element.17.refs_0_), channel_id=1, source_target_pairs={{0,2},{2,0},{4,6},{6,4},{8,10},{10,8},{12,14},{14,12},{1,3},{3,1},... | collective-permute-start | bytes 393224 | tf_op jit(solution)/shard_map/ppermute | solution.py:23
  15.1 1.9 %collective-permute-done.6.refs_1_.refs_3_ = f32[272,128]{1,0:T(8,128)S(1)} collective-permute-done((f32[272,128]{1,0:T(8,128)S(1)}, f32[272,128]{1,0:T(8,128)S(1)}, u32[]{:S(2)}, u32[]{:S(2)}) %collective-permute-start.6) | collective-permute-done | bytes 139296 | tf_op jit(solution)/shard_map/ppermute | solution.py:23
  17.0 0.2 shard_map.50.refs_5_.refs_0_.refs_1_
  17.3 0.4 collective-permute-start.10
  17.6 0.0 collective-permute-done.2.refs_2_.refs_3_
  17.7 0.2 shard_map.51.refs_5_.refs_0_.refs_1_
  17.9 1.4 %collective-permute-start.8 = (f32[256,128]{1,0:T(8,128)S(1)}, f32[256,128]{1,0:T(8,128)S(1)}, u32[]{:S(2)}, u32[]{:S(2)}) collective-permute-start(f32[256,128]{1,0:T(8,128)S(1)} %shard_map.51.refs_5_.refs_0_.refs_1_), channel_id=1, source_target_pairs={{0,4},{2,6},{4,0},{6,2},{8,12},{10,14},{12,8},{14,10},{1,5},{3,7},... | collective-permute-start | bytes 393224 | tf_op jit(solution)/shard_map/ppermute | solution.py:23
  19.3 2.0 %collective-permute-done.5.refs_2_.refs_3_ = f32[256,128]{1,0:T(8,128)S(1)} collective-permute-done((f32[256,128]{1,0:T(8,128)S(1)}, f32[256,128]{1,0:T(8,128)S(1)}, u32[]{:S(2)}, u32[]{:S(2)}) %collective-permute-start.5) | collective-permute-done | bytes 131104 | tf_op jit(solution)/shard_map/ppermute | solution.py:23
  21.3 0.2 shard_map.52.refs_5_.refs_0_.refs_1_
  21.6 0.1 collective-permute-start.9
  21.6 0.0 collective-permute-done.1.refs_2_
  21.6 0.2 shard_map.53.refs_4_.refs_0_
  21.9 1.3 %collective-permute-start.7 = (f32[256,128]{1,0:T(8,128)S(1)}, f32[256,128]{1,0:T(8,128)S(1)}, u32[]{:S(2)}, u32[]{:S(2)}) collective-permute-start(f32[256,128]{1,0:T(8,128)S(1)} %shard_map.53.refs_4_.refs_0_), channel_id=1, source_target_pairs={{0,4},{2,6},{4,0},{6,2},{8,12},{10,14},{12,8},{14,10},{1,5},{3,7},... | collective-permute-start | bytes 393224 | tf_op jit(solution)/shard_map/ppermute | solution.py:23
  23.2 6.8 %collective-permute-done.10.refs_1_.refs_3_ = f32[272,128]{1,0:T(8,128)S(1)} collective-permute-done((f32[272,128]{1,0:T(8,128)S(1)}, f32[272,128]{1,0:T(8,128)S(1)}, u32[]{:S(2)}, u32[]{:S(2)}) %collective-permute-start.10) | collective-permute-done | bytes 139296 | tf_op jit(solution)/shard_map/ppermute | solution.py:23
  30.0 2.3 %shard_map.54 = (f32[1024,128]{1,0:T(8,128)}, f32[16,128]{1,0:T(8,128)S(1)}) custom-call(f32[272,128]{1,0:T(8,128)S(1)} %shard_map.50.refs_5_.refs_0_.refs_1_, f32[272,128]{1,0:T(8,128)S(1)} %collective-permute-done.10.refs_1_.refs_3_, s32[3,3,16]{2,1,0:T(4,128)S(1)} %copy-done.1, f32[32,128]{1,0:T(8,128)S(1)} %get-tuple-element.21.refs_3_.refs_6_, ...), custom_call_target="tpu_custom_call" | custom-call | flops 1 | bytes 1 | tf_op jit(solution)/shard_map/pallas_call | solution.py:290
  32.3 0.0 collective-permute-done.8.refs_2_.refs_3_
  32.3 0.2 shard_map.55.refs_7_.refs_0_.refs_1_
  32.5 0.1 collective-permute-start.12
  32.6 3.0 %collective-permute-done.9.refs_2_.refs_3_ = f32[256,128]{1,0:T(8,128)S(1)} collective-permute-done((f32[256,128]{1,0:T(8,128)S(1)}, f32[256,128]{1,0:T(8,128)S(1)}, u32[]{:S(2)}, u32[]{:S(2)}) %collective-permute-start.9) | collective-permute-done | bytes 131104 | tf_op jit(solution)/shard_map/ppermute | solution.py:23
  35.6 2.3 %shard_map.56 = (f32[1024,128]{1,0:T(8,128)}, f32[16,128]{1,0:T(8,128)S(1)}) custom-call(f32[256,128]{1,0:T(8,128)S(1)} %shard_map.52.refs_5_.refs_0_.refs_1_, f32[272,128]{1,0:T(8,128)S(1)} %shard_map.50.refs_5_.refs_0_.refs_1_, f32[256,128]{1,0:T(8,128)S(1)} %collective-permute-done.9.refs_2_.refs_3_, ...), custom_call_target="tpu_custom_call", output_to_operand_aliasing={{0}: (8, {})} | custom-call | flops 1 | bytes 1 | tf_op jit(solution)/shard_map/pallas_call | solution.py:290
  37.9 0.0 collective-permute-done.7.refs_2_
  37.9 0.2 shard_map.57.refs_7_.refs_0_
  38.1 0.1 collective-permute-start.11
  38.2 1.6 %collective-permute-done.12.refs_2_.refs_3_ = f32[256,128]{1,0:T(8,128)S(1)} collective-permute-done((f32[256,128]{1,0:T(8,128)S(1)}, f32[256,128]{1,0:T(8,128)S(1)}, u32[]{:S(2)}, u32[]{:S(2)}) %collective-permute-start.12) | collective-permute-done | bytes 131104 | tf_op jit(solution)/shard_map/ppermute | solution.py:23
  39.8 2.3 %shard_map.58 = (f32[1024,128]{1,0:T(8,128)}, f32[16,128]{1,0:T(8,128)S(1)}) custom-call(f32[256,128]{1,0:T(8,128)S(1)} %shard_map.55.refs_7_.refs_0_.refs_1_, f32[256,128]{1,0:T(8,128)S(1)} %shard_map.52.refs_5_.refs_0_.refs_1_, f32[256,128]{1,0:T(8,128)S(1)} %collective-permute-done.12.refs_2_.refs_3_, ...), custom_call_target="tpu_custom_call", output_to_operand_aliasing={{0}: (8, {})} | custom-call | flops 1 | bytes 1 | tf_op jit(solution)/shard_map/pallas_call | solution.py:290
  42.1 1.9 %collective-permute-done.11.refs_2_ = f32[256,128]{1,0:T(8,128)S(1)} collective-permute-done((f32[256,128]{1,0:T(8,128)S(1)}, f32[256,128]{1,0:T(8,128)S(1)}, u32[]{:S(2)}, u32[]{:S(2)}) %collective-permute-start.11) | collective-permute-done | bytes 131104 | tf_op jit(solution)/shard_map/ppermute | solution.py:23
  44.1 2.9 %shard_map.59 = (f32[1024,128]{1,0:T(8,128)}, f32[16,128]{1,0:T(8,128)}) custom-call(f32[256,128]{1,0:T(8,128)S(1)} %shard_map.57.refs_7_.refs_0_, f32[256,128]{1,0:T(8,128)S(1)} %shard_map.55.refs_7_.refs_0_.refs_1_, f32[256,128]{1,0:T(8,128)S(1)} %collective-permute-done.11.refs_2_, ...), custom_call_target="tpu_custom_call", output_to_operand_aliasing={{0}: (8, {})} | custom-call | flops 1 | bytes 1 | tf_op jit(solution)/shard_map/pallas_call | solution.py:290
  (1 shorter events, 0.0 us)
Async XLA Ops:
  0.0 1.0 %copy-start = (f32[16,8192]{1,0:T(8,128)S(1)}, f32[16,8192]{1,0:T(8,128)}, u32[]{:S(2)}) copy-start(f32[16,8192]{1,0:T(8,128)} %param.4) | copy-start | bytes 1572868
  1.0 0.7 %copy-start.3 = (s32[4,3,16]{2,0,1:T(4,128)S(1)}, s32[4,3,16]{2,0,1:T(4,128)}, u32[]{:S(2)}) copy-start(s32[4,3,16]{2,0,1:T(4,128)} %param.5) | copy-start | bytes 2308
  1.3 1.2 %copy-start.2 = (s32[16]{0:T(128)S(1)}, s32[16]{0:T(128)}, u32[]{:S(2)}) copy-start(s32[16]{0:T(128)} %widths_ref.1) | copy-start | bytes 196
  1.3 1.2 %collective-permute-start = (f32[64,128]{1,0:T(8,128)S(1)}, f32[64,128]{1,0:T(8,128)S(1)}, u32[]{:S(2)}, u32[]{:S(2)}) collective-permute-start(f32[64,128]{1,0:T(8,128)S(1)} %shard_map.46.mine_ref), channel_id=1, source_target_pairs={{0,1},{1,0},{2,3},{3,2},{4,5},{5,4},{6,7},{7,6},{8,9},{9,8},{10,11... | collective-permute-start | bytes 98312 | tf_op jit(solution)/shard_map/ppermute | solution.py:23
  2.5 7.9 %copy-start.1 = (s32[3,3,16]{2,1,0:T(4,128)S(1)}, s32[3,3,16]{2,1,0:T(4,128)}, u32[]{:S(2)}) copy-start(s32[3,3,16]{2,1,0:T(4,128)} %refs_5_.5) | copy-start | bytes 1732
  3.7 6.8 %collective-permute-start.4 = (f32[288,128]{1,0:T(8,128)S(1)}, f32[288,128]{1,0:T(8,128)S(1)}, u32[]{:S(2)}, u32[]{:S(2)}) collective-permute-start(f32[288,128]{1,0:T(8,128)S(1)} %get-tuple-element.20.refs_0_.refs_1_), channel_id=1, source_target_pairs={{0,2},{2,0},{4,6},{6,4},{8,10},{10,8},{12,14},{14,12},{1,3},{3,1},... | collective-permute-start | bytes 442376 | tf_op jit(solution)/shard_map/ppermute | solution.py:23
  5.2 7.6 %collective-permute-start.3 = (f32[256,128]{1,0:T(8,128)S(1)}, f32[256,128]{1,0:T(8,128)S(1)}, u32[]{:S(2)}, u32[]{:S(2)}) collective-permute-start(f32[256,128]{1,0:T(8,128)S(1)} %get-tuple-element.19.refs_0_.refs_1_), channel_id=1, source_target_pairs={{0,2},{2,0},{4,6},{6,4},{8,10},{10,8},{12,14},{14,12},{1,3},{3,1},... | collective-permute-start | bytes 393224 | tf_op jit(solution)/shard_map/ppermute | solution.py:23
  10.7 6.3 %collective-permute-start.6 = (f32[272,128]{1,0:T(8,128)S(1)}, f32[272,128]{1,0:T(8,128)S(1)}, u32[]{:S(2)}, u32[]{:S(2)}) collective-permute-start(f32[272,128]{1,0:T(8,128)S(1)} %shard_map.48.refs_5_.refs_0_.refs_1_), channel_id=1, source_target_pairs={{0,4},{2,6},{4,0},{6,2},{8,12},{10,14},{12,8},{14,10},{1,5},{3,7},... | collective-permute-start | bytes 417800 | tf_op jit(solution)/shard_map/ppermute | solution.py:23
  11.2 6.5 %collective-permute-start.2 = (f32[256,128]{1,0:T(8,128)S(1)}, f32[256,128]{1,0:T(8,128)S(1)}, u32[]{:S(2)}, u32[]{:S(2)}) collective-permute-start(f32[256,128]{1,0:T(8,128)S(1)} %get-tuple-element.18.refs_0_.refs_1_), channel_id=1, source_target_pairs={{0,2},{2,0},{4,6},{6,4},{8,10},{10,8},{12,14},{14,12},{1,3},{3,1},... | collective-permute-start | bytes 393224 | tf_op jit(solution)/shard_map/ppermute | solution.py:23
  13.0 8.3 %collective-permute-start.5 = (f32[256,128]{1,0:T(8,128)S(1)}, f32[256,128]{1,0:T(8,128)S(1)}, u32[]{:S(2)}, u32[]{:S(2)}) collective-permute-start(f32[256,128]{1,0:T(8,128)S(1)} %shard_map.49.refs_3_.refs_0_.refs_1_), channel_id=1, source_target_pairs={{0,4},{2,6},{4,0},{6,2},{8,12},{10,14},{12,8},{14,10},{1,5},{3,7},... | collective-permute-start | bytes 393224 | tf_op jit(solution)/shard_map/ppermute | solution.py:23
  14.6 7.1 %collective-permute-start.1 = (f32[256,128]{1,0:T(8,128)S(1)}, f32[256,128]{1,0:T(8,128)S(1)}, u32[]{:S(2)}, u32[]{:S(2)}) collective-permute-start(f32[256,128]{1,0:T(8,128)S(1)} %get-tuple-element.17.refs_0_), channel_id=1, source_target_pairs={{0,2},{2,0},{4,6},{6,4},{8,10},{10,8},{12,14},{14,12},{1,3},{3,1},... | collective-permute-start | bytes 393224 | tf_op jit(solution)/shard_map/ppermute | solution.py:23
  17.3 12.7 %collective-permute-start.10 = (f32[272,128]{1,0:T(8,128)S(1)}, f32[272,128]{1,0:T(8,128)S(1)}, u32[]{:S(2)}, u32[]{:S(2)}) collective-permute-start(f32[272,128]{1,0:T(8,128)S(1)} %shard_map.50.refs_5_.refs_0_.refs_1_), channel_id=1, source_target_pairs={{0,8},{2,10},{4,12},{6,14},{8,0},{10,2},{12,4},{14,6},{1,9},{3,11}... | collective-permute-start | bytes 417800 | tf_op jit(solution)/shard_map/ppermute | solution.py:23
  17.9 14.4 %collective-permute-start.8 = (f32[256,128]{1,0:T(8,128)S(1)}, f32[256,128]{1,0:T(8,128)S(1)}, u32[]{:S(2)}, u32[]{:S(2)}) collective-permute-start(f32[256,128]{1,0:T(8,128)S(1)} %shard_map.51.refs_5_.refs_0_.refs_1_), channel_id=1, source_target_pairs={{0,4},{2,6},{4,0},{6,2},{8,12},{10,14},{12,8},{14,10},{1,5},{3,7},... | collective-permute-start | bytes 393224 | tf_op jit(solution)/shard_map/ppermute | solution.py:23
  21.6 14.1 %collective-permute-start.9 = (f32[256,128]{1,0:T(8,128)S(1)}, f32[256,128]{1,0:T(8,128)S(1)}, u32[]{:S(2)}, u32[]{:S(2)}) collective-permute-start(f32[256,128]{1,0:T(8,128)S(1)} %shard_map.52.refs_5_.refs_0_.refs_1_), channel_id=1, source_target_pairs={{0,8},{2,10},{4,12},{6,14},{8,0},{10,2},{12,4},{14,6},{1,9},{3,11}... | collective-permute-start | bytes 393224 | tf_op jit(solution)/shard_map/ppermute | solution.py:23
  21.9 16.0 %collective-permute-start.7 = (f32[256,128]{1,0:T(8,128)S(1)}, f32[256,128]{1,0:T(8,128)S(1)}, u32[]{:S(2)}, u32[]{:S(2)}) collective-permute-start(f32[256,128]{1,0:T(8,128)S(1)} %shard_map.53.refs_4_.refs_0_), channel_id=1, source_target_pairs={{0,4},{2,6},{4,0},{6,2},{8,12},{10,14},{12,8},{14,10},{1,5},{3,7},... | collective-permute-start | bytes 393224 | tf_op jit(solution)/shard_map/ppermute | solution.py:23
  32.5 7.3 %collective-permute-start.12 = (f32[256,128]{1,0:T(8,128)S(1)}, f32[256,128]{1,0:T(8,128)S(1)}, u32[]{:S(2)}, u32[]{:S(2)}) collective-permute-start(f32[256,128]{1,0:T(8,128)S(1)} %shard_map.55.refs_7_.refs_0_.refs_1_), channel_id=1, source_target_pairs={{0,8},{2,10},{4,12},{6,14},{8,0},{10,2},{12,4},{14,6},{1,9},{3,11}... | collective-permute-start | bytes 393224 | tf_op jit(solution)/shard_map/ppermute | solution.py:23
  38.1 5.9 %collective-permute-start.11 = (f32[256,128]{1,0:T(8,128)S(1)}, f32[256,128]{1,0:T(8,128)S(1)}, u32[]{:S(2)}, u32[]{:S(2)}) collective-permute-start(f32[256,128]{1,0:T(8,128)S(1)} %shard_map.57.refs_7_.refs_0_), channel_id=1, source_target_pairs={{0,8},{2,10},{4,12},{6,14},{8,0},{10,2},{12,4},{14,6},{1,9},{3,11}... | collective-permute-start | bytes 393224 | tf_op jit(solution)/shard_map/ppermute | solution.py:23

commit v4 on v3

--- a/solution.py
+++ b/solution.py
@@ -94,15 +94,20 @@
             msg_ref[pl.ds(2 * ch + (group * plan.lead + i) * 8, 8), :] = x_ref[pl.ds(base + 8 * i, 8), :]
 
 
-def local_kernel(plan, stride, x_ref, mine_ref, other_ref, delays_ref, widths_ref, *rest):
-    outs, (caps_ref, stat, first, second) = rest[: len(plan.chunks)], rest[len(plan.chunks) :]
-    width = lax.broadcasted_iota(jnp.int32, (WMAX, LANES), 0) + 1
-    caps = jnp.full((WMAX, LANES), -jnp.inf, jnp.float32)
-    for k in range(widths_ref.shape[0]):
-        caps = jnp.where(width == widths_ref[k], jnp.inf, caps)
-    caps_ref[...] = caps
+def local_kernel(plan, begin, end, stride, x_ref, mine_ref, other_ref, delays_ref, widths_ref, *rest):
     ch, rows, lead = plan.channels, plan.rows, plan.lead
+    ending = end == rows
+    here = [c for c, (start, _) in enumerate(plan.chunks) if begin <= start < end]
+    rest = rest if ending else rest[1:]
+    outs = dict(zip(here, rest))
+    stat, first, second = rest[-3:]
     half = rows * LANES
+    if not ending:
+        width = lax.broadcasted_iota(jnp.int32, (WMAX, LANES), 0) + 1
+        caps = jnp.full((WMAX, LANES), -jnp.inf, jnp.float32)
+        for k in range(widths_ref.shape[0]):
+            caps = jnp.where(width == widths_ref[k], jnp.inf, caps)
+        rest[len(here)][...] = caps
     mean_a, mean_b = mine_ref[pl.ds(0, ch), :], other_ref[pl.ds(0, ch), :]
     gap = mean_a - mean_b
     spread = mine_ref[pl.ds(ch, ch), :] + other_ref[pl.ds(ch, ch), :] + gap * gap * (half / 2.0)
@@ -115,19 +120,19 @@
         group, s = r // 8, r % 8
         mean = jnp.broadcast_to(stat[pl.ds(r, 1), :], (8, LANES))
         gain = jnp.broadcast_to(stat[pl.ds(ch + r, 1), :], (8, LANES))
-        for k in range(rows // 8):
+        for k in range(begin // 8, min(end + 8, rows) // 8):
             tile = x_ref[pl.ds(group * rows * 8 + 64 * k + s, 8, stride=8), :]
-            first[pl.ds(r * stride + 8 * k, 8), :] = (tile - mean) * gain
-        for i in range(lead):
+            first[pl.ds(r * stride + 8 * k - begin, 8), :] = (tile - mean) * gain
+        for i in range(lead if ending else 0):
             row = other_ref[pl.ds(2 * ch + (group * lead + i) * 8 + s, 1), :]
-            first[pl.ds(r * stride + rows + i, 1), :] = (row - mean[:1]) * (gain[:1] * keep)
+            first[pl.ds(r * stride + rows - begin + i, 1), :] = (row - mean[:1]) * (gain[:1] * keep)
 
     lane = lanes()
     source, target = first, second
     for level in range(plan.local_levels):
         size = 2**level
         final = level == plan.local_levels - 1
-        tiles = (rows + up(lead, 8)) // 8
+        tiles = (end - begin + (up(lead, 8) if ending else 0 if final else 8)) // 8
         jobs = table(delays_ref, level, ch)
         for r, (low, high, delay) in enumerate(jobs):
             base = r // (2 * size) * (2 * size)
@@ -140,17 +145,17 @@
                 if not final:
                     target[pl.ds(r * stride + 8 * k, 8), :] = tile
                 else:
-                    put(plan, outs, 0, r, k, tile)
+                    put(plan, outs, 0, r, k + begin // 8, tile)
         source, target = target, source
 
 
 def put(plan, outs, level, r, k, tile):
     for c, (start, stop) in enumerate(plan.chunks):
-        if start <= 8 * k < stop:
+        if start <= 8 * k < stop and c in outs:
             outs[c][pl.ds(r * (stop - start) + 8 * k - start, 8), :] = tile
     for i in range(8):
         past = 8 * k + i - plan.rows
-        if 0 <= past < plan.ext[level]:
+        if 0 <= past < plan.ext[level] and 0 in outs:
             at = plan.channels * plan.count(0) + past * plan.channels + r
             outs[0][pl.ds(at, 1), :] = tile[i : i + 1]
 
@@ -202,20 +207,19 @@
     gather_rows(plan, c, level, stride, both, own_ref, own_next, got_ref, got_next)
     lane = lanes()
     rows = n + (up(plan.ext[level + 1], 8) if c == 0 else 0)
-    outs = [None] * len(plan.chunks)
-    outs[c] = out_ref
+    outs = {c: out_ref}
     for r in range(plan.channels):
         for k in range(rows // 8):
             tile = merged_tile(plan, level, both, jobs[r], k, lane)
             put(plan, outs, level + 1, r, k + plan.chunks[c][0] // 8, tile)
 
 
-def boxcars(count, n, pitch, scale, series, caps_ref, box, lane):
+def boxcars(begin, count, n, pitch, scale, series, caps_ref, box, lane):
     tiles = n // 8
-    together = max(d for d in (1, 2, 4, 8) if d * tiles <= 8 or d == 1)
+    together = max(d for d in (1, 2, 4, 8) if d * tiles <= 16 or d == 1)
 
     def some_rows(step, carry):
-        places = [(step * together + i, k) for i in range(together) for k in range(tiles)]
+        places = [(begin + step * together + i, k) for i in range(together) for k in range(tiles)]
         here = [series[pl.ds(r * pitch + 8 * k, 8), :] for r, k in places]
         after = [series[pl.ds(r * pitch + 8 * k + 1, 8), :] for r, k in places]
         running = here
@@ -261,18 +265,16 @@
         if c > 0:
             series[pl.ds(r * pitch + n, 1), :] = after_ref[pl.ds(r, 1), :]
 
-    boxcars(ch, n, pitch, scale, series, caps_ref, box, lane)
     start = plan.chunks[c][0]
-    copies = [
-        pltpu.make_async_copy(
+    copies = []
+    for group in range(ch // 8):
+        boxcars(8 * group, 8, n, pitch, scale, series, caps_ref, box, lane)
+        copies.append(pltpu.make_async_copy(
             box.at[pl.ds(group * n * 8, n * 8), :],
             out_ref.at[pl.ds((group * plan.rows + start) * 8, n * 8), :],
             sem.at[group],
-        )
-        for group in range(ch // 8)
-    ]
-    for copy in copies:
-        copy.start()
+        ))
+        copies[-1].start()
     for copy in copies:
         copy.wait()
 
@@ -307,13 +309,20 @@
         functools.partial(stats_kernel, plan), (x,), [VMEM], [f32(2 * ch + ch * plan.lead, LANES)], [VMEM], [],
     )
     other = swap(msg, "tm", 1)
-    stride = rows + up(plan.lead, 8) + 8
-    *first, caps = call(
-        functools.partial(local_kernel, plan, stride), (x, msg, other, local_delays, widths),
-        [VMEM, VMEM, VMEM, VMEM, VMEM], [*(f32(plan.message_rows(c, 0), LANES) for c in chunks), f32(WMAX, LANES)],
-        [VMEM for _ in range(len(chunks) + 1)],
-        [pltpu.VMEM((2 * ch, LANES), jnp.float32)] + [pltpu.VMEM((ch * stride, LANES), jnp.float32)] * 2,
-    )
+    split = plan.chunks[0][0]
+    ins, first = [x, msg, other, local_delays, widths], []
+    for begin, end in ((split, rows), (0, split)):
+        stride = end - begin + up(plan.lead, 8) + 16
+        outs = [f32(plan.message_rows(c, 0), LANES) for c in chunks if begin <= plan.chunks[c][0] < end]
+        outs += [] if end == rows else [f32(WMAX, LANES)]
+        made = call(
+            functools.partial(local_kernel, plan, begin, end, stride), ins, [VMEM] * 5 + [ANY] * (len(ins) - 5),
+            outs, [VMEM] * len(outs),
+            [pltpu.VMEM((2 * ch, LANES), jnp.float32)] + [pltpu.VMEM((ch * stride, LANES), jnp.float32)] * 2,
+        )
+        first += made
+        ins = [*ins, made[0]]
+    caps = first.pop()
     held, got = {}, {}
     for c in chunks:
         held[0, c] = first[c]

time: 47.1 us -> 46.5 us (0.987)
  waiting for transfers between devices: 22.8 us -> 22 us
    ppermute x13, waiting for transfers between devices: 22.8 us -> 22 us  [swap(): return lax.ppermute(value, axis, pairs)]
    pallas_call x14 -> x15, Pallas kernels: 13 us -> 13.2 us  [call(): pl.pallas_call(kernel, in_specs=specs, out_shape=outs, out_specs=out_spec...]
  transfers between devices with their start and end apart: 13 -> 13, of which waited for: 9 -> 9; matrix products, arithmetic and copies ran while one was open for 0% -> 0% of each run, Pallas kernels for 19% -> 20%
where the time goes in v4:
time: 46.5 us; the launch traced here: 46.3 us
  waiting for transfers between devices  22 us (47%)
  Pallas kernels  13.2 us (28%)
  starting transfers between devices  9.57 us (21%)
  local copies, waits for them, and re-layouts  1.5 us (3%)
    ppermute x13, waiting for transfers between devices, swap(): return lax.ppermute(value, axis, pairs)  22 us
    pallas_call x15, Pallas kernels, call(): pl.pallas_call(kernel, in_specs=specs, out_shape=outs, out_specs=out_spec...  13.2 us
    ppermute x13, starting transfers between devices, swap(): return lax.ppermute(value, axis, pairs)  9.57 us
    unnamed x9, local copies, waits for them, and re-layouts  1.5 us
  transfers between devices with their start and end apart: 13, of which 9 were waited for; matrix products, arithmetic and copies ran while one was open for 0% of the time, Pallas kernels for 20%

profile of v4, /device:TPU:24, one launch (start us, length us, event | category | flops | bytes accessed | tf_op | source)
XLA Modules:
  0.0 46.3 jit_solution(11631859069037152083)
XLA Ops:
  0.0 0.0 copy-start
  0.0 1.0 %copy-done = f32[16,8192]{1,0:T(8,128)S(1)} copy-done((f32[16,8192]{1,0:T(8,128)S(1)}, f32[16,8192]{1,0:T(8,128)}, u32[]{:S(2)}) %copy-start) | copy-done | bytes 524312
  1.0 0.0 copy-start.3
  1.0 0.2 shard_map.46.mine_ref
  1.3 0.0 copy-start.2
  1.3 0.0 collective-permute-start
  1.3 0.4 copy-done.3
  1.7 0.7 %collective-permute-done.other_ref = f32[64,128]{1,0:T(8,128)S(1)} collective-permute-done((f32[64,128]{1,0:T(8,128)S(1)}, f32[64,128]{1,0:T(8,128)S(1)}, u32[]{:S(2)}, u32[]{:S(2)}) %collective-permute-start) | collective-permute-done | bytes 32800 | tf_op jit(solution)/shard_map/ppermute | solution.py:23
  2.5 0.0 copy-done.2
  2.5 0.8 %shard_map.47.rest_0_.refs_0_.refs_1_ = f32[288,128]{1,0:T(8,128)S(1)} custom-call(f32[1024,128]{1,0:T(8,128)S(1)} %bitcast.11, f32[64,128]{1,0:T(8,128)S(1)} %shard_map.46.mine_ref, f32[64,128]{1,0:T(8,128)S(1)} %collective-permute-done.other_ref, s32[4,3,16]{2,1,0:T(4,128)S(1)} %copy.9.delays_ref, s32[16]{0:T(128)S(1)} %copy-done.2), custom_call_target="tpu_custom_call" | custom-call | flops 1 | bytes 1 | tf_op jit(solution)/shard_map/pallas_call | solution.py:292
  3.3 1.6 %collective-permute-start.4 = (f32[288,128]{1,0:T(8,128)S(1)}, f32[288,128]{1,0:T(8,128)S(1)}, u32[]{:S(2)}, u32[]{:S(2)}) collective-permute-start(f32[288,128]{1,0:T(8,128)S(1)} %shard_map.47.rest_0_.refs_0_.refs_1_), channel_id=1, source_target_pairs={{0,2},{2,0},{4,6},{6,4},{8,10},{10,8},{12,14},{14,12},{1,3},{3,1},... | collective-permute-start | bytes 442376 | tf_op jit(solution)/shard_map/ppermute | solution.py:23
  4.8 1.0 %shard_map.48 = (f32[256,128]{1,0:T(8,128)S(1)}, f32[256,128]{1,0:T(8,128)S(1)}, f32[256,128]{1,0:T(8,128)S(1)}, f32[32,128]{1,0:T(8,128)S(1)}) custom-call(f32[1024,128]{1,0:T(8,128)S(1)} %bitcast.12, f32[64,128]{1,0:T(8,128)S(1)} %shard_map.46.mine_ref, f32[64,128]{1,0:T(8,128)S(1)} %collective-permute-done.other_ref, s32[4,3,16]{2,1,0:T(4,128)S(1)} %copy.9.delays_ref, ...), custom_call_target="tpu_custom_call" | custom-call | flops 1 | bytes 1 | tf_op jit(solution)/shard_map/pallas_call | solution.py:292
  5.8 0.6 %collective-permute-start.3 = (f32[256,128]{1,0:T(8,128)S(1)}, f32[256,128]{1,0:T(8,128)S(1)}, u32[]{:S(2)}, u32[]{:S(2)}) collective-permute-start(f32[256,128]{1,0:T(8,128)S(1)} %get-tuple-element.18.refs_0_.refs_1_), channel_id=1, source_target_pairs={{0,2},{2,0},{4,6},{6,4},{8,10},{10,8},{12,14},{14,12},{1,3},{3,1},... | collective-permute-start | bytes 393224 | tf_op jit(solution)/shard_map/ppermute | solution.py:23
  6.4 3.6 %collective-permute-done.4.refs_1_.refs_3_ = f32[288,128]{1,0:T(8,128)S(1)} collective-permute-done((f32[288,128]{1,0:T(8,128)S(1)}, f32[288,128]{1,0:T(8,128)S(1)}, u32[]{:S(2)}, u32[]{:S(2)}) %collective-permute-start.4) | collective-permute-done | bytes 147488 | tf_op jit(solution)/shard_map/ppermute | solution.py:23
  10.0 0.0 copy-done.1
  10.0 0.3 shard_map.49.refs_5_.refs_0_.refs_1_
  10.3 0.5 %collective-permute-start.6 = (f32[272,128]{1,0:T(8,128)S(1)}, f32[272,128]{1,0:T(8,128)S(1)}, u32[]{:S(2)}, u32[]{:S(2)}) collective-permute-start(f32[272,128]{1,0:T(8,128)S(1)} %shard_map.49.refs_5_.refs_0_.refs_1_), channel_id=1, source_target_pairs={{0,4},{2,6},{4,0},{6,2},{8,12},{10,14},{12,8},{14,10},{1,5},{3,7},... | collective-permute-start | bytes 417800 | tf_op jit(solution)/shard_map/ppermute | solution.py:23
  10.8 1.5 %collective-permute-start.2 = (f32[256,128]{1,0:T(8,128)S(1)}, f32[256,128]{1,0:T(8,128)S(1)}, u32[]{:S(2)}, u32[]{:S(2)}) collective-permute-start(f32[256,128]{1,0:T(8,128)S(1)} %get-tuple-element.17.refs_0_.refs_1_), channel_id=1, source_target_pairs={{0,2},{2,0},{4,6},{6,4},{8,10},{10,8},{12,14},{14,12},{1,3},{3,1},... | collective-permute-start | bytes 393224 | tf_op jit(solution)/shard_map/ppermute | solution.py:23
  12.3 0.1 collective-permute-done.3.refs_2_.refs_3_
  12.4 0.2 shard_map.50.refs_3_.refs_0_.refs_1_
  12.6 1.5 %collective-permute-start.5 = (f32[256,128]{1,0:T(8,128)S(1)}, f32[256,128]{1,0:T(8,128)S(1)}, u32[]{:S(2)}, u32[]{:S(2)}) collective-permute-start(f32[256,128]{1,0:T(8,128)S(1)} %shard_map.50.refs_3_.refs_0_.refs_1_), channel_id=1, source_target_pairs={{0,4},{2,6},{4,0},{6,2},{8,12},{10,14},{12,8},{14,10},{1,5},{3,7},... | collective-permute-start | bytes 393224 | tf_op jit(solution)/shard_map/ppermute | solution.py:23
  14.2 0.5 %collective-permute-start.1 = (f32[256,128]{1,0:T(8,128)S(1)}, f32[256,128]{1,0:T(8,128)S(1)}, u32[]{:S(2)}, u32[]{:S(2)}) collective-permute-start(f32[256,128]{1,0:T(8,128)S(1)} %get-tuple-element.16.refs_0_), channel_id=1, source_target_pairs={{0,2},{2,0},{4,6},{6,4},{8,10},{10,8},{12,14},{14,12},{1,3},{3,1},... | collective-permute-start | bytes 393224 | tf_op jit(solution)/shard_map/ppermute | solution.py:23
  14.7 1.9 %collective-permute-done.6.refs_1_.refs_3_ = f32[272,128]{1,0:T(8,128)S(1)} collective-permute-done((f32[272,128]{1,0:T(8,128)S(1)}, f32[272,128]{1,0:T(8,128)S(1)}, u32[]{:S(2)}, u32[]{:S(2)}) %collective-permute-start.6) | collective-permute-done | bytes 139296 | tf_op jit(solution)/shard_map/ppermute | solution.py:23
  16.6 0.2 shard_map.51.refs_5_.refs_0_.refs_1_
  16.9 0.4 collective-permute-start.10
  17.3 0.0 collective-permute-done.2.refs_2_.refs_3_
  17.3 0.2 shard_map.52.refs_5_.refs_0_.refs_1_
  17.5 1.4 %collective-permute-start.8 = (f32[256,128]{1,0:T(8,128)S(1)}, f32[256,128]{1,0:T(8,128)S(1)}, u32[]{:S(2)}, u32[]{:S(2)}) collective-permute-start(f32[256,128]{1,0:T(8,128)S(1)} %shard_map.52.refs_5_.refs_0_.refs_1_), channel_id=1, source_target_pairs={{0,4},{2,6},{4,0},{6,2},{8,12},{10,14},{12,8},{14,10},{1,5},{3,7},... | collective-permute-start | bytes 393224 | tf_op jit(solution)/shard_map/ppermute | solution.py:23
  19.0 2.0 %collective-permute-done.5.refs_2_.refs_3_ = f32[256,128]{1,0:T(8,128)S(1)} collective-permute-done((f32[256,128]{1,0:T(8,128)S(1)}, f32[256,128]{1,0:T(8,128)S(1)}, u32[]{:S(2)}, u32[]{:S(2)}) %collective-permute-start.5) | collective-permute-done | bytes 131104 | tf_op jit(solution)/shard_map/ppermute | solution.py:23
  20.9 0.2 shard_map.53.refs_5_.refs_0_.refs_1_
  21.2 0.1 collective-permute-start.9
  21.2 0.0 collective-permute-done.1.refs_2_
  21.3 0.2 shard_map.54.refs_4_.refs_0_
  21.5 1.3 %collective-permute-start.7 = (f32[256,128]{1,0:T(8,128)S(1)}, f32[256,128]{1,0:T(8,128)S(1)}, u32[]{:S(2)}, u32[]{:S(2)}) collective-permute-start(f32[256,128]{1,0:T(8,128)S(1)} %shard_map.54.refs_4_.refs_0_), channel_id=1, source_target_pairs={{0,4},{2,6},{4,0},{6,2},{8,12},{10,14},{12,8},{14,10},{1,5},{3,7},... | collective-permute-start | bytes 393224 | tf_op jit(solution)/shard_map/ppermute | solution.py:23
  22.8 6.8 %collective-permute-done.10.refs_1_.refs_3_ = f32[272,128]{1,0:T(8,128)S(1)} collective-permute-done((f32[272,128]{1,0:T(8,128)S(1)}, f32[272,128]{1,0:T(8,128)S(1)}, u32[]{:S(2)}, u32[]{:S(2)}) %collective-permute-start.10) | collective-permute-done | bytes 139296 | tf_op jit(solution)/shard_map/ppermute | solution.py:23
  29.6 2.2 %shard_map.55 = (f32[1024,128]{1,0:T(8,128)}, f32[16,128]{1,0:T(8,128)S(1)}) custom-call(f32[272,128]{1,0:T(8,128)S(1)} %shard_map.51.refs_5_.refs_0_.refs_1_, f32[272,128]{1,0:T(8,128)S(1)} %collective-permute-done.10.refs_1_.refs_3_, s32[3,3,16]{2,1,0:T(4,128)S(1)} %copy-done.1, f32[32,128]{1,0:T(8,128)S(1)} %get-tuple-element.19.refs_3_.refs_6_, ...), custom_call_target="tpu_custom_call" | custom-call | flops 1 | bytes 1 | tf_op jit(solution)/shard_map/pallas_call | solution.py:292
  31.8 0.0 collective-permute-done.8.refs_2_.refs_3_
  31.8 0.2 shard_map.56.refs_7_.refs_0_.refs_1_
  32.0 0.1 collective-permute-start.12
  32.1 3.1 %collective-permute-done.9.refs_2_.refs_3_ = f32[256,128]{1,0:T(8,128)S(1)} collective-permute-done((f32[256,128]{1,0:T(8,128)S(1)}, f32[256,128]{1,0:T(8,128)S(1)}, u32[]{:S(2)}, u32[]{:S(2)}) %collective-permute-start.9) | collective-permute-done | bytes 131104 | tf_op jit(solution)/shard_map/ppermute | solution.py:23
  35.2 2.1 %shard_map.57 = (f32[1024,128]{1,0:T(8,128)}, f32[16,128]{1,0:T(8,128)S(1)}) custom-call(f32[256,128]{1,0:T(8,128)S(1)} %shard_map.53.refs_5_.refs_0_.refs_1_, f32[272,128]{1,0:T(8,128)S(1)} %shard_map.51.refs_5_.refs_0_.refs_1_, f32[256,128]{1,0:T(8,128)S(1)} %collective-permute-done.9.refs_2_.refs_3_, ...), custom_call_target="tpu_custom_call", output_to_operand_aliasing={{0}: (8, {})} | custom-call | flops 1 | bytes 1 | tf_op jit(solution)/shard_map/pallas_call | solution.py:292
  37.4 0.0 collective-permute-done.7.refs_2_
  37.4 0.2 shard_map.58.refs_7_.refs_0_
  37.6 0.1 collective-permute-start.11
  37.7 1.7 %collective-permute-done.12.refs_2_.refs_3_ = f32[256,128]{1,0:T(8,128)S(1)} collective-permute-done((f32[256,128]{1,0:T(8,128)S(1)}, f32[256,128]{1,0:T(8,128)S(1)}, u32[]{:S(2)}, u32[]{:S(2)}) %collective-permute-start.12) | collective-permute-done | bytes 131104 | tf_op jit(solution)/shard_map/ppermute | solution.py:23
  39.4 2.1 %shard_map.59 = (f32[1024,128]{1,0:T(8,128)}, f32[16,128]{1,0:T(8,128)S(1)}) custom-call(f32[256,128]{1,0:T(8,128)S(1)} %shard_map.56.refs_7_.refs_0_.refs_1_, f32[256,128]{1,0:T(8,128)S(1)} %shard_map.53.refs_5_.refs_0_.refs_1_, f32[256,128]{1,0:T(8,128)S(1)} %collective-permute-done.12.refs_2_.refs_3_, ...), custom_call_target="tpu_custom_call", output_to_operand_aliasing={{0}: (8, {})} | custom-call | flops 1 | bytes 1 | tf_op jit(solution)/shard_map/pallas_call | solution.py:292
  41.6 2.0 %collective-permute-done.11.refs_2_ = f32[256,128]{1,0:T(8,128)S(1)} collective-permute-done((f32[256,128]{1,0:T(8,128)S(1)}, f32[256,128]{1,0:T(8,128)S(1)}, u32[]{:S(2)}, u32[]{:S(2)}) %collective-permute-start.11) | collective-permute-done | bytes 131104 | tf_op jit(solution)/shard_map/ppermute | solution.py:23
  43.6 2.7 %shard_map.60 = (f32[1024,128]{1,0:T(8,128)}, f32[16,128]{1,0:T(8,128)}) custom-call(f32[256,128]{1,0:T(8,128)S(1)} %shard_map.58.refs_7_.refs_0_, f32[256,128]{1,0:T(8,128)S(1)} %shard_map.56.refs_7_.refs_0_.refs_1_, f32[256,128]{1,0:T(8,128)S(1)} %collective-permute-done.11.refs_2_, ...), custom_call_target="tpu_custom_call", output_to_operand_aliasing={{0}: (8, {})} | custom-call | flops 1 | bytes 1 | tf_op jit(solution)/shard_map/pallas_call | solution.py:292
  (2 shorter events, 0.0 us)
Async XLA Ops:
  0.0 1.0 %copy-start = (f32[16,8192]{1,0:T(8,128)S(1)}, f32[16,8192]{1,0:T(8,128)}, u32[]{:S(2)}) copy-start(f32[16,8192]{1,0:T(8,128)} %param.4) | copy-start | bytes 1572868
  1.0 0.7 %copy-start.3 = (s32[4,3,16]{2,0,1:T(4,128)S(1)}, s32[4,3,16]{2,0,1:T(4,128)}, u32[]{:S(2)}) copy-start(s32[4,3,16]{2,0,1:T(4,128)} %param.5) | copy-start | bytes 2308
  1.3 1.2 %copy-start.2 = (s32[16]{0:T(128)S(1)}, s32[16]{0:T(128)}, u32[]{:S(2)}) copy-start(s32[16]{0:T(128)} %widths_ref.3) | copy-start | bytes 196
  1.3 1.2 %collective-permute-start = (f32[64,128]{1,0:T(8,128)S(1)}, f32[64,128]{1,0:T(8,128)S(1)}, u32[]{:S(2)}, u32[]{:S(2)}) collective-permute-start(f32[64,128]{1,0:T(8,128)S(1)} %shard_map.46.mine_ref), channel_id=1, source_target_pairs={{0,1},{1,0},{2,3},{3,2},{4,5},{5,4},{6,7},{7,6},{8,9},{9,8},{10,11... | collective-permute-start | bytes 98312 | tf_op jit(solution)/shard_map/ppermute | solution.py:23
  3.3 6.8 %collective-permute-start.4 = (f32[288,128]{1,0:T(8,128)S(1)}, f32[288,128]{1,0:T(8,128)S(1)}, u32[]{:S(2)}, u32[]{:S(2)}) collective-permute-start(f32[288,128]{1,0:T(8,128)S(1)} %shard_map.47.rest_0_.refs_0_.refs_1_), channel_id=1, source_target_pairs={{0,2},{2,0},{4,6},{6,4},{8,10},{10,8},{12,14},{14,12},{1,3},{3,1},... | collective-permute-start | bytes 442376 | tf_op jit(solution)/shard_map/ppermute | solution.py:23
  4.8 5.2 %copy-start.1 = (s32[3,3,16]{2,1,0:T(4,128)S(1)}, s32[3,3,16]{2,1,0:T(4,128)}, u32[]{:S(2)}) copy-start(s32[3,3,16]{2,1,0:T(4,128)} %refs_5_.5) | copy-start | bytes 1732
  5.8 6.6 %collective-permute-start.3 = (f32[256,128]{1,0:T(8,128)S(1)}, f32[256,128]{1,0:T(8,128)S(1)}, u32[]{:S(2)}, u32[]{:S(2)}) collective-permute-start(f32[256,128]{1,0:T(8,128)S(1)} %get-tuple-element.18.refs_0_.refs_1_), channel_id=1, source_target_pairs={{0,2},{2,0},{4,6},{6,4},{8,10},{10,8},{12,14},{14,12},{1,3},{3,1},... | collective-permute-start | bytes 393224 | tf_op jit(solution)/shard_map/ppermute | solution.py:23
  10.3 6.3 %collective-permute-start.6 = (f32[272,128]{1,0:T(8,128)S(1)}, f32[272,128]{1,0:T(8,128)S(1)}, u32[]{:S(2)}, u32[]{:S(2)}) collective-permute-start(f32[272,128]{1,0:T(8,128)S(1)} %shard_map.49.refs_5_.refs_0_.refs_1_), channel_id=1, source_target_pairs={{0,4},{2,6},{4,0},{6,2},{8,12},{10,14},{12,8},{14,10},{1,5},{3,7},... | collective-permute-start | bytes 417800 | tf_op jit(solution)/shard_map/ppermute | solution.py:23
  10.8 6.5 %collective-permute-start.2 = (f32[256,128]{1,0:T(8,128)S(1)}, f32[256,128]{1,0:T(8,128)S(1)}, u32[]{:S(2)}, u32[]{:S(2)}) collective-permute-start(f32[256,128]{1,0:T(8,128)S(1)} %get-tuple-element.17.refs_0_.refs_1_), channel_id=1, source_target_pairs={{0,2},{2,0},{4,6},{6,4},{8,10},{10,8},{12,14},{14,12},{1,3},{3,1},... | collective-permute-start | bytes 393224 | tf_op jit(solution)/shard_map/ppermute | solution.py:23
  12.6 8.3 %collective-permute-start.5 = (f32[256,128]{1,0:T(8,128)S(1)}, f32[256,128]{1,0:T(8,128)S(1)}, u32[]{:S(2)}, u32[]{:S(2)}) collective-permute-start(f32[256,128]{1,0:T(8,128)S(1)} %shard_map.50.refs_3_.refs_0_.refs_1_), channel_id=1, source_target_pairs={{0,4},{2,6},{4,0},{6,2},{8,12},{10,14},{12,8},{14,10},{1,5},{3,7},... | collective-permute-start | bytes 393224 | tf_op jit(solution)/shard_map/ppermute | solution.py:23
  14.2 7.1 %collective-permute-start.1 = (f32[256,128]{1,0:T(8,128)S(1)}, f32[256,128]{1,0:T(8,128)S(1)}, u32[]{:S(2)}, u32[]{:S(2)}) collective-permute-start(f32[256,128]{1,0:T(8,128)S(1)} %get-tuple-element.16.refs_0_), channel_id=1, source_target_pairs={{0,2},{2,0},{4,6},{6,4},{8,10},{10,8},{12,14},{14,12},{1,3},{3,1},... | collective-permute-start | bytes 393224 | tf_op jit(solution)/shard_map/ppermute | solution.py:23
  16.9 12.7 %collective-permute-start.10 = (f32[272,128]{1,0:T(8,128)S(1)}, f32[272,128]{1,0:T(8,128)S(1)}, u32[]{:S(2)}, u32[]{:S(2)}) collective-permute-start(f32[272,128]{1,0:T(8,128)S(1)} %shard_map.51.refs_5_.refs_0_.refs_1_), channel_id=1, source_target_pairs={{0,8},{2,10},{4,12},{6,14},{8,0},{10,2},{12,4},{14,6},{1,9},{3,11}... | collective-permute-start | bytes 417800 | tf_op jit(solution)/shard_map/ppermute | solution.py:23
  17.5 14.3 %collective-permute-start.8 = (f32[256,128]{1,0:T(8,128)S(1)}, f32[256,128]{1,0:T(8,128)S(1)}, u32[]{:S(2)}, u32[]{:S(2)}) collective-permute-start(f32[256,128]{1,0:T(8,128)S(1)} %shard_map.52.refs_5_.refs_0_.refs_1_), channel_id=1, source_target_pairs={{0,4},{2,6},{4,0},{6,2},{8,12},{10,14},{12,8},{14,10},{1,5},{3,7},... | collective-permute-start | bytes 393224 | tf_op jit(solution)/shard_map/ppermute | solution.py:23
  21.2 14.1 %collective-permute-start.9 = (f32[256,128]{1,0:T(8,128)S(1)}, f32[256,128]{1,0:T(8,128)S(1)}, u32[]{:S(2)}, u32[]{:S(2)}) collective-permute-start(f32[256,128]{1,0:T(8,128)S(1)} %shard_map.53.refs_5_.refs_0_.refs_1_), channel_id=1, source_target_pairs={{0,8},{2,10},{4,12},{6,14},{8,0},{10,2},{12,4},{14,6},{1,9},{3,11}... | collective-permute-start | bytes 393224 | tf_op jit(solution)/shard_map/ppermute | solution.py:23
  21.5 15.9 %collective-permute-start.7 = (f32[256,128]{1,0:T(8,128)S(1)}, f32[256,128]{1,0:T(8,128)S(1)}, u32[]{:S(2)}, u32[]{:S(2)}) collective-permute-start(f32[256,128]{1,0:T(8,128)S(1)} %shard_map.54.refs_4_.refs_0_), channel_id=1, source_target_pairs={{0,4},{2,6},{4,0},{6,2},{8,12},{10,14},{12,8},{14,10},{1,5},{3,7},... | collective-permute-start | bytes 393224 | tf_op jit(solution)/shard_map/ppermute | solution.py:23
  32.0 7.4 %collective-permute-start.12 = (f32[256,128]{1,0:T(8,128)S(1)}, f32[256,128]{1,0:T(8,128)S(1)}, u32[]{:S(2)}, u32[]{:S(2)}) collective-permute-start(f32[256,128]{1,0:T(8,128)S(1)} %shard_map.56.refs_7_.refs_0_.refs_1_), channel_id=1, source_target_pairs={{0,8},{2,10},{4,12},{6,14},{8,0},{10,2},{12,4},{14,6},{1,9},{3,11}... | collective-permute-start | bytes 393224 | tf_op jit(solution)/shard_map/ppermute | solution.py:23
  37.6 5.9 %collective-permute-start.11 = (f32[256,128]{1,0:T(8,128)S(1)}, f32[256,128]{1,0:T(8,128)S(1)}, u32[]{:S(2)}, u32[]{:S(2)}) collective-permute-start(f32[256,128]{1,0:T(8,128)S(1)} %shard_map.58.refs_7_.refs_0_), channel_id=1, source_target_pairs={{0,8},{2,10},{4,12},{6,14},{8,0},{10,2},{12,4},{14,6},{1,9},{3,11}... | collective-permute-start | bytes 393224 | tf_op jit(solution)/shard_map/ppermute | solution.py:23

commit v5 on v4

--- a/solution.py
+++ b/solution.py
@@ -12,6 +12,7 @@
 LANES = 128
 EPSILON = 1e-05
 SHARES = (2, 2, 2, 2)
+LAST = (2, 2, 2, 1, 1)
 
 
 def up(value, by):
@@ -44,7 +45,7 @@
 
 
 class Plan:
-    def __init__(self, channels, block_len, freq_count, tm_count):
+    def __init__(self, channels, block_len, freq_count, tm_count, shares=SHARES):
         self.channels = channels
         self.rows = block_len // LANES
         self.freq_count = freq_count
@@ -52,9 +53,9 @@
         self.local_levels = channels.bit_length() - 1
         self.levels = freq_count.bit_length() - 1
         tiles = self.rows // 8
-        total = sum(SHARES)
-        ends = [tiles - tiles * sum(SHARES[:i]) // total for i in range(len(SHARES) + 1)]
-        self.chunks = [(8 * ends[i + 1], 8 * ends[i]) for i in range(len(SHARES))]
+        total = sum(shares)
+        ends = [tiles - tiles * sum(shares[:i]) // total for i in range(len(shares) + 1)]
+        self.chunks = [(8 * ends[i + 1], 8 * ends[i]) for i in range(len(shares))]
         reach = WMAX - 1
         need = [reach]
         for level in reversed(range(self.levels)):
@@ -196,22 +197,22 @@
     )
 
 
-def merge_kernel(plan, c, level, stride, *refs):
+def merge_kernel(plan, target, parts, c, level, stride, *refs):
     if c == 0:
-        own_ref, got_ref, delays_ref, _, out_ref, both = refs
+        own_ref, got_ref, delays_ref, _, *out_refs, both = refs
         own_next = got_next = None
     else:
-        own_ref, own_next, got_ref, got_next, delays_ref, _, out_ref, both = refs
+        own_ref, own_next, got_ref, got_next, delays_ref, _, *out_refs, both = refs
     n = plan.count(c)
     jobs = merge_jobs(plan, level, stride, delays_ref)
     gather_rows(plan, c, level, stride, both, own_ref, own_next, got_ref, got_next)
     lane = lanes()
     rows = n + (up(plan.ext[level + 1], 8) if c == 0 else 0)
-    outs = {c: out_ref}
+    outs = dict(zip(parts, out_refs))
     for r in range(plan.channels):
         for k in range(rows // 8):
             tile = merged_tile(plan, level, both, jobs[r], k, lane)
-            put(plan, outs, level + 1, r, k + plan.chunks[c][0] // 8, tile)
+            put(target, outs, level + 1, r, k + plan.chunks[c][0] // 8, tile)
 
 
 def boxcars(begin, count, n, pitch, scale, series, caps_ref, box, lane):
@@ -301,7 +302,7 @@
     )(*ins)
 
 
-def per_device(plan, spectra, local_delays, merge_delays, widths):
+def per_device(plan, fine, spectra, local_delays, merge_delays, widths):
     ch, rows = plan.channels, plan.rows
     chunks = range(len(plan.chunks))
     x = spectra.reshape(ch // 8, 8, rows, LANES).transpose(0, 2, 1, 3).reshape(ch * rows, LANES)
@@ -328,9 +329,15 @@
         held[0, c] = first[c]
         got[0, c] = swap(first[c], "freq", 1)
     last, head, result = caps, None, None
-    for level, c in sorted(((level, c) for level in range(plan.levels) for c in chunks), key=turn(plan)):
+    top = plan.levels - 1
+    if any(fine.count(c) < up(ch * 2**top // LANES + 1, 8) for c in range(len(fine.chunks))):
+        fine = plan
+    jobs = [(level, c) for level in range(top) for c in chunks]
+    jobs += [(top, c) for c in range(len(fine.chunks))]
+    for level, c in sorted(jobs, key=turn(plan)):
         if True:
-            n = plan.count(c)
+            used = fine if level == top else plan
+            n = used.count(c)
             span = ch * 2**level
             ahead = span // LANES + 1
             tail = max((up(plan.ext[level + 1], 8) if c == 0 else 0) + ahead, plan.ext[level], up(ahead, 8))
@@ -340,12 +347,18 @@
             ins = [group[level, i] for group in (held, got) for i in near]
             specs = [VMEM] * len(ins)
             if level < plan.levels - 1:
-                (last,) = call(
-                    functools.partial(merge_kernel, plan, c, level, stride), (*ins, merge_delays, last),
-                    [*specs, VMEM, ANY], [f32(plan.message_rows(c, level + 1), LANES)], [VMEM], [both],
+                target = fine if level + 1 == top else plan
+                start, stop = plan.chunks[c]
+                parts = [i for i, (a, _) in enumerate(target.chunks) if start <= a < stop]
+                made = call(
+                    functools.partial(merge_kernel, plan, target, parts, c, level, stride),
+                    (*ins, merge_delays, last), [*specs, VMEM, ANY],
+                    [f32(target.message_rows(i, level + 1), LANES) for i in parts], [VMEM] * len(parts), [both],
                 )
-                held[level + 1, c] = last
-                got[level + 1, c] = swap(last, "freq", 2 ** (level + 1))
+                last = made[0]
+                for i, message in zip(parts, made):
+                    held[level + 1, i] = message
+                    got[level + 1, i] = swap(message, "freq", 2 ** (level + 1))
                 continue
             if c > 0:
                 ins, specs = [*ins, head], [*specs, VMEM]
@@ -355,7 +368,7 @@
                 aliases = {len(ins): 0}
                 ins, specs = [*ins, result], [*specs, ANY]
             result, head = call(
-                functools.partial(final_kernel, plan, c, stride), ins, specs,
+                functools.partial(final_kernel, fine, c, stride), ins, specs,
                 [f32(ch * rows, LANES), f32(ch, LANES)], [ANY, VMEM],
                 [both, pltpu.VMEM((ch * (n + 8), LANES), jnp.float32),
                  pltpu.VMEM((ch * n, LANES), jnp.float32), pltpu.SemaphoreType.DMA((ch // 8,))], aliases,
@@ -371,8 +384,9 @@
         channels = spectra.shape[0] // (mesh.shape["beam"] * mesh.shape["freq"])
         block_len = spectra.shape[1] // mesh.shape["tm"]
         plan = Plan(channels, block_len, mesh.shape["freq"], mesh.shape["tm"])
+        fine = Plan(channels, block_len, mesh.shape["freq"], mesh.shape["tm"], LAST)
         return jax.shard_map(
-            functools.partial(per_device, plan), mesh=mesh, in_specs=placed,
+            functools.partial(per_device, plan, fine), mesh=mesh, in_specs=placed,
             out_specs=P(("beam", "freq"), "tm"), check_vma=False,
         )(spectra, local_delays, merge_delays, widths)
 

time: 46.5 us -> 47.7 us (1.026)
  the two profiles are of different devices: /device:TPU:24 before, /device:TPU:8 now
where the time goes in v5:
time: 47.7 us; the launch traced here: 47.5 us
  starting transfers between devices  22.4 us (47%)
  Pallas kernels  14 us (29%)
  waiting for transfers between devices  9.57 us (20%)
  local copies, waits for them, and re-layouts  1.5 us (3%)
    ppermute x14, starting transfers between devices, swap(): return lax.ppermute(value, axis, pairs)  22.4 us
    pallas_call x16, Pallas kernels, call(): pl.pallas_call(kernel, in_specs=specs, out_shape=outs, out_specs=out_spec...  14 us
    ppermute x14, waiting for transfers between devices, swap(): return lax.ppermute(value, axis, pairs)  9.57 us
    unnamed x9, local copies, waits for them, and re-layouts  1.5 us
  transfers between devices with their start and end apart: 14, of which 5 were waited for; matrix products, arithmetic and copies ran while one was open for 0% of the time, Pallas kernels for 23%

profile of v5, /device:TPU:8, one launch (start us, length us, event | category | flops | bytes accessed | tf_op | source)
XLA Modules:
  0.0 47.5 jit_solution(15422717738541440266)
XLA Ops:
  0.0 1.0 %copy-done = f32[16,8192]{1,0:T(8,128)S(1)} copy-done((f32[16,8192]{1,0:T(8,128)S(1)}, f32[16,8192]{1,0:T(8,128)}, u32[]{:S(2)}) %copy-start) | copy-done | bytes 524312
  1.0 0.2 shard_map.46.mine_ref
  1.3 0.0 collective-permute-start
  1.3 0.4 copy-done.3
  1.7 0.7 %collective-permute-done.other_ref = f32[64,128]{1,0:T(8,128)S(1)} collective-permute-done((f32[64,128]{1,0:T(8,128)S(1)}, f32[64,128]{1,0:T(8,128)S(1)}, u32[]{:S(2)}, u32[]{:S(2)}) %collective-permute-start) | collective-permute-done | bytes 32800 | tf_op jit(solution)/shard_map/ppermute | solution.py:24
  2.5 0.0 copy-done.2
  2.5 0.8 %shard_map.47.rest_0_.refs_0_.refs_1_ = f32[288,128]{1,0:T(8,128)S(1)} custom-call(f32[1024,128]{1,0:T(8,128)S(1)} %bitcast.11, f32[64,128]{1,0:T(8,128)S(1)} %shard_map.46.mine_ref, f32[64,128]{1,0:T(8,128)S(1)} %collective-permute-done.other_ref, s32[4,3,16]{2,1,0:T(4,128)S(1)} %copy.10.delays_ref, s32[16]{0:T(128)S(1)} %copy-done.2), custom_call_target="tpu_custom_call" | custom-call | flops 1 | bytes 1 | tf_op jit(solution)/shard_map/pallas_call | solution.py:293
  3.3 1.6 %collective-permute-start.4 = (f32[288,128]{1,0:T(8,128)S(1)}, f32[288,128]{1,0:T(8,128)S(1)}, u32[]{:S(2)}, u32[]{:S(2)}) collective-permute-start(f32[288,128]{1,0:T(8,128)S(1)} %shard_map.47.rest_0_.refs_0_.refs_1_), channel_id=1, source_target_pairs={{0,2},{2,0},{4,6},{6,4},{8,10},{10,8},{12,14},{14,12},{1,3},{3,1},... | collective-permute-start | bytes 442376 | tf_op jit(solution)/shard_map/ppermute | solution.py:24
  4.8 1.0 %shard_map.48 = (f32[256,128]{1,0:T(8,128)S(1)}, f32[256,128]{1,0:T(8,128)S(1)}, f32[256,128]{1,0:T(8,128)S(1)}, f32[32,128]{1,0:T(8,128)S(1)}) custom-call(f32[1024,128]{1,0:T(8,128)S(1)} %bitcast.12, f32[64,128]{1,0:T(8,128)S(1)} %shard_map.46.mine_ref, f32[64,128]{1,0:T(8,128)S(1)} %collective-permute-done.other_ref, s32[4,3,16]{2,1,0:T(4,128)S(1)} %copy.10.delays_ref, ...), custom_call_target="tpu_custom_call" | custom-call | flops 1 | bytes 1 | tf_op jit(solution)/shard_map/pallas_call | solution.py:293
  5.8 0.6 %collective-permute-start.3 = (f32[256,128]{1,0:T(8,128)S(1)}, f32[256,128]{1,0:T(8,128)S(1)}, u32[]{:S(2)}, u32[]{:S(2)}) collective-permute-start(f32[256,128]{1,0:T(8,128)S(1)} %get-tuple-element.22.refs_0_.refs_1_), channel_id=1, source_target_pairs={{0,2},{2,0},{4,6},{6,4},{8,10},{10,8},{12,14},{14,12},{1,3},{3,1},... | collective-permute-start | bytes 393224 | tf_op jit(solution)/shard_map/ppermute | solution.py:24
  6.4 3.6 %collective-permute-done.4.refs_1_.refs_3_ = f32[288,128]{1,0:T(8,128)S(1)} collective-permute-done((f32[288,128]{1,0:T(8,128)S(1)}, f32[288,128]{1,0:T(8,128)S(1)}, u32[]{:S(2)}, u32[]{:S(2)}) %collective-permute-start.4) | collective-permute-done | bytes 147488 | tf_op jit(solution)/shard_map/ppermute | solution.py:24
  10.0 0.0 copy-done.1
  10.0 0.3 shard_map.49.refs_5_.refs_0_.refs_1_
  10.3 0.1 collective-permute-start.6
  10.4 1.9 %collective-permute-start.2 = (f32[256,128]{1,0:T(8,128)S(1)}, f32[256,128]{1,0:T(8,128)S(1)}, u32[]{:S(2)}, u32[]{:S(2)}) collective-permute-start(f32[256,128]{1,0:T(8,128)S(1)} %get-tuple-element.21.refs_0_.refs_1_), channel_id=1, source_target_pairs={{0,2},{2,0},{4,6},{6,4},{8,10},{10,8},{12,14},{14,12},{1,3},{3,1},... | collective-permute-start | bytes 393224 | tf_op jit(solution)/shard_map/ppermute | solution.py:24
  12.3 0.0 collective-permute-done.3.refs_2_.refs_3_
  12.3 0.2 shard_map.50.refs_3_.refs_0_.refs_1_
  12.6 1.6 %collective-permute-start.5 = (f32[256,128]{1,0:T(8,128)S(1)}, f32[256,128]{1,0:T(8,128)S(1)}, u32[]{:S(2)}, u32[]{:S(2)}) collective-permute-start(f32[256,128]{1,0:T(8,128)S(1)} %shard_map.50.refs_3_.refs_0_.refs_1_), channel_id=1, source_target_pairs={{0,4},{2,6},{4,0},{6,2},{8,12},{10,14},{12,8},{14,10},{1,5},{3,7},... | collective-permute-start | bytes 393224 | tf_op jit(solution)/shard_map/ppermute | solution.py:24
  14.2 0.5 %collective-permute-start.1 = (f32[256,128]{1,0:T(8,128)S(1)}, f32[256,128]{1,0:T(8,128)S(1)}, u32[]{:S(2)}, u32[]{:S(2)}) collective-permute-start(f32[256,128]{1,0:T(8,128)S(1)} %get-tuple-element.20.refs_0_), channel_id=1, source_target_pairs={{0,2},{2,0},{4,6},{6,4},{8,10},{10,8},{12,14},{14,12},{1,3},{3,1},... | collective-permute-start | bytes 393224 | tf_op jit(solution)/shard_map/ppermute | solution.py:24
  14.7 1.9 %collective-permute-done.6.refs_1_.refs_3_ = f32[272,128]{1,0:T(8,128)S(1)} collective-permute-done((f32[272,128]{1,0:T(8,128)S(1)}, f32[272,128]{1,0:T(8,128)S(1)}, u32[]{:S(2)}, u32[]{:S(2)}) %collective-permute-start.6) | collective-permute-done | bytes 139296 | tf_op jit(solution)/shard_map/ppermute | solution.py:24
  16.6 0.2 shard_map.51.refs_5_.refs_0_.refs_1_
  16.9 2.7 %collective-permute-start.10 = (f32[272,128]{1,0:T(8,128)S(1)}, f32[272,128]{1,0:T(8,128)S(1)}, u32[]{:S(2)}, u32[]{:S(2)}) collective-permute-start(f32[272,128]{1,0:T(8,128)S(1)} %shard_map.51.refs_5_.refs_0_.refs_1_), channel_id=1, source_target_pairs={{0,8},{2,10},{4,12},{6,14},{8,0},{10,2},{12,4},{14,6},{1,9},{3,11}... | collective-permute-start | bytes 417800 | tf_op jit(solution)/shard_map/ppermute | solution.py:24
  19.5 0.0 collective-permute-done.2.refs_2_.refs_3_
  19.5 0.2 shard_map.52.refs_5_.refs_0_.refs_1_
  19.8 0.5 collective-permute-start.8
  20.3 0.0 collective-permute-done.5.refs_2_.refs_3_
  20.3 0.2 shard_map.53.refs_5_.refs_0_.refs_1_
  20.5 3.3 %collective-permute-start.9 = (f32[256,128]{1,0:T(8,128)S(1)}, f32[256,128]{1,0:T(8,128)S(1)}, u32[]{:S(2)}, u32[]{:S(2)}) collective-permute-start(f32[256,128]{1,0:T(8,128)S(1)} %shard_map.53.refs_5_.refs_0_.refs_1_), channel_id=1, source_target_pairs={{0,8},{2,10},{4,12},{6,14},{8,0},{10,2},{12,4},{14,6},{1,9},{3,11}... | collective-permute-start | bytes 393224 | tf_op jit(solution)/shard_map/ppermute | solution.py:24
  23.8 0.0 collective-permute-done.1.refs_2_
  23.8 0.2 shard_map.54.refs_4_.refs_0_
  24.1 0.1 collective-permute-start.7
  24.1 1.8 %collective-permute-done.10.refs_1_.refs_3_ = f32[272,128]{1,0:T(8,128)S(1)} collective-permute-done((f32[272,128]{1,0:T(8,128)S(1)}, f32[272,128]{1,0:T(8,128)S(1)}, u32[]{:S(2)}, u32[]{:S(2)}) %collective-permute-start.10) | collective-permute-done | bytes 139296 | tf_op jit(solution)/shard_map/ppermute | solution.py:24
  26.0 2.2 %shard_map.55 = (f32[1024,128]{1,0:T(8,128)}, f32[16,128]{1,0:T(8,128)S(1)}) custom-call(f32[272,128]{1,0:T(8,128)S(1)} %shard_map.51.refs_5_.refs_0_.refs_1_, f32[272,128]{1,0:T(8,128)S(1)} %collective-permute-done.10.refs_1_.refs_3_, s32[3,3,16]{2,1,0:T(4,128)S(1)} %copy-done.1, f32[32,128]{1,0:T(8,128)S(1)} %get-tuple-element.23.refs_3_.refs_6_, ...), custom_call_target="tpu_custom_call" | custom-call | flops 1 | bytes 1 | tf_op jit(solution)/shard_map/pallas_call | solution.py:293
  28.1 0.0 collective-permute-done.8.refs_2_.refs_3_
  28.2 0.2 shard_map.56.refs_7_.refs_0_.refs_1_
  28.4 6.3 %collective-permute-start.13 = (f32[256,128]{1,0:T(8,128)S(1)}, f32[256,128]{1,0:T(8,128)S(1)}, u32[]{:S(2)}, u32[]{:S(2)}) collective-permute-start(f32[256,128]{1,0:T(8,128)S(1)} %shard_map.56.refs_7_.refs_0_.refs_1_), channel_id=1, source_target_pairs={{0,8},{2,10},{4,12},{6,14},{8,0},{10,2},{12,4},{14,6},{1,9},{3,11}... | collective-permute-start | bytes 393224 | tf_op jit(solution)/shard_map/ppermute | solution.py:24
  34.7 0.0 collective-permute-done.9.refs_2_.refs_3_
  34.7 2.1 %shard_map.57 = (f32[1024,128]{1,0:T(8,128)}, f32[16,128]{1,0:T(8,128)S(1)}) custom-call(f32[256,128]{1,0:T(8,128)S(1)} %shard_map.53.refs_5_.refs_0_.refs_1_, f32[272,128]{1,0:T(8,128)S(1)} %shard_map.51.refs_5_.refs_0_.refs_1_, f32[256,128]{1,0:T(8,128)S(1)} %collective-permute-done.9.refs_2_.refs_3_, ...), custom_call_target="tpu_custom_call", output_to_operand_aliasing={{0}: (8, {})} | custom-call | flops 1 | bytes 1 | tf_op jit(solution)/shard_map/pallas_call | solution.py:293
  36.8 0.0 collective-permute-done.7.refs_2_
  36.9 0.3 shard_map.58
  37.1 3.2 %collective-permute-start.12 = (f32[128,128]{1,0:T(8,128)S(1)}, f32[128,128]{1,0:T(8,128)S(1)}, u32[]{:S(2)}, u32[]{:S(2)}) collective-permute-start(f32[128,128]{1,0:T(8,128)S(1)} %get-tuple-element.28.refs_7_.refs_0_.refs_1_), channel_id=1, source_target_pairs={{0,8},{2,10},{4,12},{6,14},{8,0},{10,2},{12,4},{14,6},{1,9},{3,11}... | collective-permute-start | bytes 196616 | tf_op jit(solution)/shard_map/ppermute | solution.py:24
  40.3 0.1 collective-permute-start.11
  40.4 0.0 collective-permute-done.13.refs_2_.refs_3_
  40.4 2.1 %shard_map.59 = (f32[1024,128]{1,0:T(8,128)}, f32[16,128]{1,0:T(8,128)S(1)}) custom-call(f32[256,128]{1,0:T(8,128)S(1)} %shard_map.56.refs_7_.refs_0_.refs_1_, f32[256,128]{1,0:T(8,128)S(1)} %shard_map.53.refs_5_.refs_0_.refs_1_, f32[256,128]{1,0:T(8,128)S(1)} %collective-permute-done.13.refs_2_.refs_3_, ...), custom_call_target="tpu_custom_call", output_to_operand_aliasing={{0}: (8, {})} | custom-call | flops 1 | bytes 1 | tf_op jit(solution)/shard_map/pallas_call | solution.py:293
  42.5 0.0 collective-permute-done.12.refs_2_.refs_3_
  42.5 1.5 %shard_map.60 = (f32[1024,128]{1,0:T(8,128)}, f32[16,128]{1,0:T(8,128)S(1)}) custom-call(f32[128,128]{1,0:T(8,128)S(1)} %get-tuple-element.28.refs_7_.refs_0_.refs_1_, f32[256,128]{1,0:T(8,128)S(1)} %shard_map.56.refs_7_.refs_0_.refs_1_, f32[128,128]{1,0:T(8,128)S(1)} %collective-permute-done.12.refs_2_.refs_3_, ...), custom_call_target="tpu_custom_call", output_to_operand_aliasing={{0}: (8, {})} | custom-call | flops 1 | bytes 1 | tf_op jit(solution)/shard_map/pallas_call | solution.py:293
  44.0 1.4 %collective-permute-done.11.refs_2_ = f32[128,128]{1,0:T(8,128)S(1)} collective-permute-done((f32[128,128]{1,0:T(8,128)S(1)}, f32[128,128]{1,0:T(8,128)S(1)}, u32[]{:S(2)}, u32[]{:S(2)}) %collective-permute-start.11) | collective-permute-done | bytes 65568 | tf_op jit(solution)/shard_map/ppermute | solution.py:24
  45.5 2.1 %shard_map.61 = (f32[1024,128]{1,0:T(8,128)}, f32[16,128]{1,0:T(8,128)}) custom-call(f32[128,128]{1,0:T(8,128)S(1)} %get-tuple-element.27.refs_0_, f32[128,128]{1,0:T(8,128)S(1)} %get-tuple-element.28.refs_7_.refs_0_.refs_1_, f32[128,128]{1,0:T(8,128)S(1)} %collective-permute-done.11.refs_2_, ...), custom_call_target="tpu_custom_call", output_to_operand_aliasing={{0}: (8, {})} | custom-call | flops 1 | bytes 1 | tf_op jit(solution)/shard_map/pallas_call | solution.py:293
  (5 shorter events, 0.0 us)
Async XLA Ops:
  0.0 1.0 %copy-start = (f32[16,8192]{1,0:T(8,128)S(1)}, f32[16,8192]{1,0:T(8,128)}, u32[]{:S(2)}) copy-start(f32[16,8192]{1,0:T(8,128)} %param.4) | copy-start | bytes 1572868
  1.0 0.7 %copy-start.3 = (s32[4,3,16]{2,0,1:T(4,128)S(1)}, s32[4,3,16]{2,0,1:T(4,128)}, u32[]{:S(2)}) copy-start(s32[4,3,16]{2,0,1:T(4,128)} %param.5) | copy-start | bytes 2308
  1.3 1.2 %copy-start.2 = (s32[16]{0:T(128)S(1)}, s32[16]{0:T(128)}, u32[]{:S(2)}) copy-start(s32[16]{0:T(128)} %widths_ref.3) | copy-start | bytes 196
  1.3 1.2 %collective-permute-start = (f32[64,128]{1,0:T(8,128)S(1)}, f32[64,128]{1,0:T(8,128)S(1)}, u32[]{:S(2)}, u32[]{:S(2)}) collective-permute-start(f32[64,128]{1,0:T(8,128)S(1)} %shard_map.46.mine_ref), channel_id=1, source_target_pairs={{0,1},{1,0},{2,3},{3,2},{4,5},{5,4},{6,7},{7,6},{8,9},{9,8},{10,11... | collective-permute-start | bytes 98312 | tf_op jit(solution)/shard_map/ppermute | solution.py:24
  3.3 6.8 %collective-permute-start.4 = (f32[288,128]{1,0:T(8,128)S(1)}, f32[288,128]{1,0:T(8,128)S(1)}, u32[]{:S(2)}, u32[]{:S(2)}) collective-permute-start(f32[288,128]{1,0:T(8,128)S(1)} %shard_map.47.rest_0_.refs_0_.refs_1_), channel_id=1, source_target_pairs={{0,2},{2,0},{4,6},{6,4},{8,10},{10,8},{12,14},{14,12},{1,3},{3,1},... | collective-permute-start | bytes 442376 | tf_op jit(solution)/shard_map/ppermute | solution.py:24
  4.8 5.2 %copy-start.1 = (s32[3,3,16]{2,1,0:T(4,128)S(1)}, s32[3,3,16]{2,1,0:T(4,128)}, u32[]{:S(2)}) copy-start(s32[3,3,16]{2,1,0:T(4,128)} %refs_5_.7) | copy-start | bytes 1732
  5.8 6.5 %collective-permute-start.3 = (f32[256,128]{1,0:T(8,128)S(1)}, f32[256,128]{1,0:T(8,128)S(1)}, u32[]{:S(2)}, u32[]{:S(2)}) collective-permute-start(f32[256,128]{1,0:T(8,128)S(1)} %get-tuple-element.22.refs_0_.refs_1_), channel_id=1, source_target_pairs={{0,2},{2,0},{4,6},{6,4},{8,10},{10,8},{12,14},{14,12},{1,3},{3,1},... | collective-permute-start | bytes 393224 | tf_op jit(solution)/shard_map/ppermute | solution.py:24
  10.3 6.3 %collective-permute-start.6 = (f32[272,128]{1,0:T(8,128)S(1)}, f32[272,128]{1,0:T(8,128)S(1)}, u32[]{:S(2)}, u32[]{:S(2)}) collective-permute-start(f32[272,128]{1,0:T(8,128)S(1)} %shard_map.49.refs_5_.refs_0_.refs_1_), channel_id=1, source_target_pairs={{0,4},{2,6},{4,0},{6,2},{8,12},{10,14},{12,8},{14,10},{1,5},{3,7},... | collective-permute-start | bytes 417800 | tf_op jit(solution)/shard_map/ppermute | solution.py:24
  10.4 9.2 %collective-permute-start.2 = (f32[256,128]{1,0:T(8,128)S(1)}, f32[256,128]{1,0:T(8,128)S(1)}, u32[]{:S(2)}, u32[]{:S(2)}) collective-permute-start(f32[256,128]{1,0:T(8,128)S(1)} %get-tuple-element.21.refs_0_.refs_1_), channel_id=1, source_target_pairs={{0,2},{2,0},{4,6},{6,4},{8,10},{10,8},{12,14},{14,12},{1,3},{3,1},... | collective-permute-start | bytes 393224 | tf_op jit(solution)/shard_map/ppermute | solution.py:24
  12.6 7.7 %collective-permute-start.5 = (f32[256,128]{1,0:T(8,128)S(1)}, f32[256,128]{1,0:T(8,128)S(1)}, u32[]{:S(2)}, u32[]{:S(2)}) collective-permute-start(f32[256,128]{1,0:T(8,128)S(1)} %shard_map.50.refs_3_.refs_0_.refs_1_), channel_id=1, source_target_pairs={{0,4},{2,6},{4,0},{6,2},{8,12},{10,14},{12,8},{14,10},{1,5},{3,7},... | collective-permute-start | bytes 393224 | tf_op jit(solution)/shard_map/ppermute | solution.py:24
  14.2 9.6 %collective-permute-start.1 = (f32[256,128]{1,0:T(8,128)S(1)}, f32[256,128]{1,0:T(8,128)S(1)}, u32[]{:S(2)}, u32[]{:S(2)}) collective-permute-start(f32[256,128]{1,0:T(8,128)S(1)} %get-tuple-element.20.refs_0_), channel_id=1, source_target_pairs={{0,2},{2,0},{4,6},{6,4},{8,10},{10,8},{12,14},{14,12},{1,3},{3,1},... | collective-permute-start | bytes 393224 | tf_op jit(solution)/shard_map/ppermute | solution.py:24
  16.9 9.1 %collective-permute-start.10 = (f32[272,128]{1,0:T(8,128)S(1)}, f32[272,128]{1,0:T(8,128)S(1)}, u32[]{:S(2)}, u32[]{:S(2)}) collective-permute-start(f32[272,128]{1,0:T(8,128)S(1)} %shard_map.51.refs_5_.refs_0_.refs_1_), channel_id=1, source_target_pairs={{0,8},{2,10},{4,12},{6,14},{8,0},{10,2},{12,4},{14,6},{1,9},{3,11}... | collective-permute-start | bytes 417800 | tf_op jit(solution)/shard_map/ppermute | solution.py:24
  19.8 8.4 %collective-permute-start.8 = (f32[256,128]{1,0:T(8,128)S(1)}, f32[256,128]{1,0:T(8,128)S(1)}, u32[]{:S(2)}, u32[]{:S(2)}) collective-permute-start(f32[256,128]{1,0:T(8,128)S(1)} %shard_map.52.refs_5_.refs_0_.refs_1_), channel_id=1, source_target_pairs={{0,4},{2,6},{4,0},{6,2},{8,12},{10,14},{12,8},{14,10},{1,5},{3,7},... | collective-permute-start | bytes 393224 | tf_op jit(solution)/shard_map/ppermute | solution.py:24
  20.5 14.2 %collective-permute-start.9 = (f32[256,128]{1,0:T(8,128)S(1)}, f32[256,128]{1,0:T(8,128)S(1)}, u32[]{:S(2)}, u32[]{:S(2)}) collective-permute-start(f32[256,128]{1,0:T(8,128)S(1)} %shard_map.53.refs_5_.refs_0_.refs_1_), channel_id=1, source_target_pairs={{0,8},{2,10},{4,12},{6,14},{8,0},{10,2},{12,4},{14,6},{1,9},{3,11}... | collective-permute-start | bytes 393224 | tf_op jit(solution)/shard_map/ppermute | solution.py:24
  24.1 12.8 %collective-permute-start.7 = (f32[256,128]{1,0:T(8,128)S(1)}, f32[256,128]{1,0:T(8,128)S(1)}, u32[]{:S(2)}, u32[]{:S(2)}) collective-permute-start(f32[256,128]{1,0:T(8,128)S(1)} %shard_map.54.refs_4_.refs_0_), channel_id=1, source_target_pairs={{0,4},{2,6},{4,0},{6,2},{8,12},{10,14},{12,8},{14,10},{1,5},{3,7},... | collective-permute-start | bytes 393224 | tf_op jit(solution)/shard_map/ppermute | solution.py:24
  28.4 12.0 %collective-permute-start.13 = (f32[256,128]{1,0:T(8,128)S(1)}, f32[256,128]{1,0:T(8,128)S(1)}, u32[]{:S(2)}, u32[]{:S(2)}) collective-permute-start(f32[256,128]{1,0:T(8,128)S(1)} %shard_map.56.refs_7_.refs_0_.refs_1_), channel_id=1, source_target_pairs={{0,8},{2,10},{4,12},{6,14},{8,0},{10,2},{12,4},{14,6},{1,9},{3,11}... | collective-permute-start | bytes 393224 | tf_op jit(solution)/shard_map/ppermute | solution.py:24
  37.1 5.4 %collective-permute-start.12 = (f32[128,128]{1,0:T(8,128)S(1)}, f32[128,128]{1,0:T(8,128)S(1)}, u32[]{:S(2)}, u32[]{:S(2)}) collective-permute-start(f32[128,128]{1,0:T(8,128)S(1)} %get-tuple-element.28.refs_7_.refs_0_.refs_1_), channel_id=1, source_target_pairs={{0,8},{2,10},{4,12},{6,14},{8,0},{10,2},{12,4},{14,6},{1,9},{3,11}... | collective-permute-start | bytes 196616 | tf_op jit(solution)/shard_map/ppermute | solution.py:24
  40.3 5.2 %collective-permute-start.11 = (f32[128,128]{1,0:T(8,128)S(1)}, f32[128,128]{1,0:T(8,128)S(1)}, u32[]{:S(2)}, u32[]{:S(2)}) collective-permute-start(f32[128,128]{1,0:T(8,128)S(1)} %get-tuple-element.27.refs_0_), channel_id=1, source_target_pairs={{0,8},{2,10},{4,12},{6,14},{8,0},{10,2},{12,4},{14,6},{1,9},{3,11}... | collective-permute-start | bytes 196616 | tf_op jit(solution)/shard_map/ppermute | solution.py:24
